TPU v7x, 32 devices: a whole 2x2x4 slice. The times are simulated.
32 devices in a mesh: rows: 16 (over z, y, core), ch: 2 (over x).
Axes of the slice: x: 2, y: 2, z: 4, core: 2. Of those that a mesh axis runs over, the one named last changes fastest.
Arguments:
- inputs: bfloat16 [32, 1024, 2048], P('rows', None, 'ch'), may hold values from -6 to 6
- doc_lengths: int32 [32, 8], P('rows'), may hold values from 1 to 512, 1024 in all within a row
- layer_norm_gain: float32 [2048], P('ch'), may hold values from 0.5 to 1.5
- layer_norm_bias: float32 [2048], P('ch'), may hold values from -3 to 3
- weight: bfloat16 [2048, 3, 2048], P(None, None, 'ch'), may hold values from -0.125 to 0.125
- forget_weight: float32 [2048], P('ch'), may hold values from -1 to 1
- reset_weight: float32 [2048], P('ch'), may hold values from -1 to 1
- forget_bias: float32 [2048], P('ch'), may hold values from 0 to 4
- reset_bias: float32 [2048], P('ch'), may hold values from -1 to 1
- out_grad: bfloat16 [32, 1024, 2048], P('rows', None, 'ch'), may hold values from -6 to 6
Outputs:
- mixed: bfloat16 [32, 1024, 2048], P('rows', None, 'ch')
- input_grad: bfloat16 [32, 1024, 2048], P('rows', None, 'ch')
- final_state: float32 [32, 2048], P('rows', 'ch')
- weight_grad: float32 [2048, 3, 2048], P(None, None, 'ch')
- gain_grad: float32 [2048], P('ch')
- shift_grad: float32 [2048], P('ch')
- forget_weight_grad: float32 [2048], P('ch')
- reset_weight_grad: float32 [2048], P('ch')
- forget_bias_grad: float32 [2048], P('ch')
- reset_bias_grad: float32 [2048], P('ch')
Inputs may be any that keep to these rules, and one draw needn't show every extreme that they name: `doc_lengths`: each row's 8 lengths sum to 1024, and the longest document of every row has exactly 512 tokens.
All inputs are finite; a program needn't handle non-finite values.
Results may differ from a plain program's by a relative error of at most 0.0091.
Values may be sent and summed in bfloat16 or wider, within the bound.
A program may use at most 320 MiB of HBM per device.

v0:
```python
import functools

import jax
import jax.numpy as jnp
from jax import lax
from jax.experimental import pallas as pl
from jax.experimental.pallas import tpu as pltpu
from jax.sharding import PartitionSpec as P

MESH = pl.DeviceIdType.MESH
F32 = jnp.float32
BF16 = jnp.bfloat16
EPSILON = 1e-05
LANES = 128
SUBLANES = 8
PROJECT_TOKENS = 128
RECUR_TOKENS = 64
GROUP = 16
ANY = pl.BlockSpec(memory_space=pl.ANY)
VMEM_LIMIT = 60 * 1024 * 1024


def project_kernel(
    x_ref, params_ref, weight_ref,
    u_ref, normed_t_ref, mean_ref, scale_ref,
    both, weights, params, normed, normed_t, mean_out, scale_out, u_out,
    send_sem, recv_sem, own_sem, param_sem, weight_sem, u_sem, t_sem, stat_sem,
):
    ch = lax.axis_index("ch")
    other = 1 - ch
    tokens, width = x_ref.shape
    full = 2 * width
    size = PROJECT_TOKENS
    chunks = tokens // size
    own_columns = pl.ds(pl.multiple_of(ch * width, width), width)

    load_weight = pltpu.make_async_copy(weight_ref, weights, weight_sem)
    load_weight.start()
    own_params = pltpu.make_async_copy(params_ref, params.at[ch], param_sem.at[0])
    own_params.start()

    barrier = pltpu.get_barrier_semaphore()
    pl.semaphore_signal(barrier, inc=1, device_id={"ch": other}, device_id_type=MESH)
    pl.semaphore_wait(barrier, 1)

    send_params = pltpu.make_async_remote_copy(
        src_ref=params_ref, dst_ref=params.at[ch], send_sem=param_sem.at[1], recv_sem=param_sem.at[2],
        device_id={"ch": other}, device_id_type=MESH,
    )
    send_params.start()

    def exchange(chunk):
        rows = pl.ds(pl.multiple_of(chunk * size, size), size)
        return pltpu.make_async_remote_copy(
            src_ref=x_ref.at[rows], dst_ref=both.at[rows, own_columns],
            send_sem=send_sem.at[chunk], recv_sem=recv_sem.at[chunk],
            device_id={"ch": other}, device_id_type=MESH,
        )

    def keep_own(chunk):
        rows = pl.ds(pl.multiple_of(chunk * size, size), size)
        return pltpu.make_async_copy(x_ref.at[rows], both.at[rows, own_columns], own_sem.at[chunk])

    def outputs(chunk, slot):
        rows = pl.ds(pl.multiple_of(chunk * size, size), size)
        return (
            pltpu.make_async_copy(u_out.at[slot], u_ref.at[:, rows], u_sem.at[slot]),
            pltpu.make_async_copy(normed_t.at[slot], normed_t_ref.at[:, rows], t_sem.at[slot]),
            pltpu.make_async_copy(mean_out.at[slot], mean_ref.at[rows], stat_sem.at[0, slot]),
            pltpu.make_async_copy(scale_out.at[slot], scale_ref.at[rows], stat_sem.at[1, slot]),
        )

    def begin(chunk, carry):
        exchange(chunk).start()
        keep_own(chunk).start()
        return carry

    lax.fori_loop(0, chunks, begin, 0)
    own_params.wait()
    send_params.wait()
    load_weight.wait()
    gain = jnp.concatenate([params[0, 0:1], params[1, 0:1]], axis=1)
    shift = jnp.concatenate([params[0, 1:2], params[1, 1:2]], axis=1)

    def work(chunk, carry):
        slot = lax.rem(chunk, 2)
        keep_own(chunk).wait()
        exchange(chunk).wait()

        @pl.when(chunk >= 2)
        def _():
            for copy in outputs(chunk - 2, slot):
                copy.wait()

        @pl.loop(0, size // GROUP)
        def _(part):
            rows = pl.ds(pl.multiple_of(chunk * size + part * GROUP, GROUP), GROUP)
            here = pl.ds(pl.multiple_of(part * GROUP, GROUP), GROUP)
            x = both[rows, :].astype(F32)
            mean = jnp.sum(x, axis=1, keepdims=True) * (1.0 / full)
            centered = x - mean
            variance = jnp.sum(centered * centered, axis=1, keepdims=True) * (1.0 / full)
            scale = lax.rsqrt(variance + EPSILON)
            normed[here, :] = (centered * scale * gain + shift).astype(BF16)
            mean_out[slot, here, :] = jnp.broadcast_to(mean, (GROUP, LANES))
            scale_out[slot, here, :] = jnp.broadcast_to(scale, (GROUP, LANES))

        for gate in range(3):
            u_out[slot, gate] = jnp.dot(normed[...], weights[gate], preferred_element_type=F32)

        @pl.loop(0, full // LANES)
        def _(part):
            columns = pl.ds(pl.multiple_of(part * LANES, LANES), LANES)
            normed_t[slot, columns, :] = normed[:, columns].T

        for copy in outputs(chunk, slot):
            copy.start()
        return carry

    lax.fori_loop(0, chunks, work, 0)
    for chunk in (chunks - 2, chunks - 1):
        for copy in outputs(chunk, chunk % 2):
            copy.wait()


def project(x, params, weight):
    tokens, width = x.shape
    full = 2 * width
    size = PROJECT_TOKENS
    chunks = tokens // size
    dma = pltpu.SemaphoreType.DMA
    return pl.pallas_call(
        project_kernel,
        out_shape=(
            jax.ShapeDtypeStruct((3, tokens, width), F32),
            jax.ShapeDtypeStruct((full, tokens), BF16),
            jax.ShapeDtypeStruct((tokens, LANES), F32),
            jax.ShapeDtypeStruct((tokens, LANES), F32),
        ),
        in_specs=[ANY] * 3,
        out_specs=[ANY] * 4,
        scratch_shapes=[
            pltpu.VMEM((tokens, full), BF16),
            pltpu.VMEM((3, full, width), BF16),
            pltpu.VMEM((2, SUBLANES, width), F32),
            pltpu.VMEM((size, full), BF16),
            pltpu.VMEM((2, full, size), BF16),
            pltpu.VMEM((2, size, LANES), F32),
            pltpu.VMEM((2, size, LANES), F32),
            pltpu.VMEM((2, 3, size, width), F32),
            dma((chunks,)), dma((chunks,)), dma((chunks,)), dma((3,)), dma, dma((2,)), dma((2,)), dma((2, 2)),
        ],
        compiler_params=pltpu.CompilerParams(
            collective_id=0, has_side_effects=True, vmem_limit_bytes=VMEM_LIMIT
        ),
        name="project",
    )(x, params, weight)


def recur_kernel(
    keep_ref, u_ref, x_ref, grad_ref, params_ref,
    mixed_ref, pass_ref, reset_ref, gates_ref, final_ref, sums_ref,
    direct_s, extra_s, forget_s, slope_s, before_s, state_s, sums_s,
):
    step = pl.program_id(0)
    rows_here, size = x_ref.shape[0], x_ref.shape[1]
    blocks = pl.num_programs(0) // 2
    width = x_ref.shape[2]
    block_forward = step
    block_back = 2 * blocks - 1 - step
    forget_weight = params_ref[0]
    reset_weight = params_ref[1]
    forget_bias = params_ref[2]
    reset_bias = params_ref[3]
    half_forget_weight = 0.5 * forget_weight
    half_reset_weight = 0.5 * reset_weight
    half_forget_bias = 0.5 * forget_bias
    half_reset_bias = 0.5 * reset_bias

    def spread(value):
        return value.astype(F32).reshape(GROUP, SUBLANES, LANES)

    def flat(parts):
        return jnp.stack(parts).reshape(GROUP, width).astype(BF16)

    @pl.when(step == 0)
    def _():
        state_s[...] = jnp.zeros_like(state_s)
        sums_s[...] = jnp.zeros_like(sums_s)

    @pl.when(step < blocks)
    def _():
        def group(index, carry):
            here = pl.ds(pl.multiple_of(index * GROUP, GROUP), GROUP)
            state = list(carry[:rows_here])
            weight_sum, bias_sum = carry[rows_here:]
            loaded = []
            for row in range(rows_here):
                loaded.append((
                    u_ref[0, row, here].reshape(GROUP, SUBLANES, LANES),
                    u_ref[1, row, here].reshape(GROUP, SUBLANES, LANES),
                    u_ref[2, row, here].reshape(GROUP, SUBLANES, LANES),
                    spread(x_ref[row, here]),
                    spread(grad_ref[row, here]),
                ))
            out = [([], [], []) for _ in range(rows_here)]
            for k in range(GROUP):
                time = block_forward * size + index * GROUP + k
                for row in range(rows_here):
                    up_x, up_f, up_r, x, grad = (part[k] for part in loaded[row])
                    before = state[row] * keep_ref[row, time]
                    bent = jnp.tanh(0.5 * up_f + half_forget_bias + half_forget_weight * before)
                    gap = before - up_x
                    after = 0.5 * (before + up_x) + bent * (0.5 * gap)
                    state[row] = after
                    forget = 0.5 * bent + 0.5
                    reset = 0.5 * jnp.tanh(0.5 * up_r + half_reset_bias + half_reset_weight * before) + 0.5
                    over = after - x
                    direct = grad * reset
                    reset_grad = direct * over * (1.0 - reset)
                    direct_s[row, time] = direct
                    extra_s[row, time] = reset_grad * reset_weight
                    forget_s[row, time] = forget
                    slope_s[row, time] = gap * forget * (1.0 - forget)
                    before_s[row, time] = before
                    weight_sum = weight_sum + reset_grad * before
                    bias_sum = bias_sum + reset_grad
                    out[row][0].append(x + reset * over)
                    out[row][1].append(grad - direct)
                    out[row][2].append(reset_grad)
            for row in range(rows_here):
                mixed_ref[row, here] = flat(out[row][0])
                pass_ref[row, here] = flat(out[row][1])
                reset_ref[row, here] = flat(out[row][2])
            return (*state, weight_sum, bias_sum)

        carry = lax.fori_loop(
            0, size // GROUP, group, (*[state_s[row] for row in range(rows_here)], sums_s[1], sums_s[3])
        )
        for row in range(rows_here):
            state_s[row] = carry[row]
        sums_s[1] = carry[rows_here]
        sums_s[3] = carry[rows_here + 1]

    @pl.when(step == blocks - 1)
    def _():
        final_ref[...] = state_s[...]
        state_s[...] = jnp.zeros_like(state_s)

    @pl.when(step >= blocks)
    def _():
        def group(turn, carry):
            index = size // GROUP - 1 - turn
            here = pl.ds(pl.multiple_of(index * GROUP, GROUP), GROUP)
            running = list(carry[:rows_here])
            weight_sum, bias_sum = carry[rows_here:]
            out = [([None] * GROUP, [None] * GROUP) for _ in range(rows_here)]
            for k in range(GROUP - 1, -1, -1):
                time = block_back * size + index * GROUP + k
                for row in range(rows_here):
                    forget = forget_s[row, time]
                    slope = slope_s[row, time]
                    keep = keep_ref[row, time]
                    state_grad = direct_s[row, time] + running[row]
                    through = (forget + slope * forget_weight) * keep
                    running[row] = through * state_grad + extra_s[row, time] * keep
                    forget_grad = state_grad * slope
                    weight_sum = weight_sum + forget_grad * before_s[row, time]
                    bias_sum = bias_sum + forget_grad
                    out[row][0][k] = state_grad - state_grad * forget
                    out[row][1][k] = forget_grad
            for row in range(rows_here):
                gates_ref[0, row, here] = flat(out[row][0])
                gates_ref[1, row, here] = flat(out[row][1])
            return (*running, weight_sum, bias_sum)

        carry = lax.fori_loop(
            0, size // GROUP, group, (*[state_s[row] for row in range(rows_here)], sums_s[0], sums_s[2])
        )
        for row in range(rows_here):
            state_s[row] = carry[row]
        sums_s[0] = carry[rows_here]
        sums_s[2] = carry[rows_here + 1]

    @pl.when(step == 2 * blocks - 1)
    def _():
        sums_ref[...] = sums_s[...]


def recur(keep, u, x, grad, params):
    rows_here, length, width = x.shape
    size = RECUR_TOKENS
    blocks = length // size
    ahead = lambda i: jnp.minimum(i, blocks - 1)
    back = lambda i: jnp.minimum(2 * blocks - 1 - i, blocks - 1)
    row_block = lambda place: pl.BlockSpec((rows_here, size, width), lambda i: (0, place(i), 0))
    whole = lambda *shape: pl.BlockSpec(shape, lambda i: (0,) * len(shape))
    tile = (SUBLANES, LANES)
    kept = pltpu.VMEM((rows_here, length) + tile, F32)
    return pl.pallas_call(
        recur_kernel,
        grid=(2 * blocks,),
        out_shape=(
            jax.ShapeDtypeStruct((rows_here, length, width), BF16),
            jax.ShapeDtypeStruct((rows_here, length, width), BF16),
            jax.ShapeDtypeStruct((rows_here, length, width), BF16),
            jax.ShapeDtypeStruct((2, rows_here, length, width), BF16),
            jax.ShapeDtypeStruct((rows_here,) + tile, F32),
            jax.ShapeDtypeStruct((4,) + tile, F32),
        ),
        in_specs=[
            pl.BlockSpec(memory_space=pltpu.SMEM),
            pl.BlockSpec((3, rows_here, size, width), lambda i: (0, 0, ahead(i), 0)),
            row_block(ahead), row_block(ahead), whole(4, *tile),
        ],
        out_specs=(
            row_block(ahead), row_block(ahead), row_block(ahead),
            pl.BlockSpec((2, rows_here, size, width), lambda i: (0, 0, back(i), 0)),
            whole(rows_here, *tile), whole(4, *tile),
        ),
        scratch_shapes=[kept] * 5 + [pltpu.VMEM((rows_here,) + tile, F32), pltpu.VMEM((4,) + tile, F32)],
        compiler_params=pltpu.CompilerParams(vmem_limit_bytes=VMEM_LIMIT),
        name="recur",
    )(keep, u, x, grad, params)


def on_device(
    inputs, doc_lengths, layer_norm_gain, layer_norm_bias, weight, forget_weight, reset_weight, forget_bias,
    reset_bias, out_grad,
):
    rows_here, length, width = inputs.shape
    full = width * lax.axis_size("ch")
    tokens = rows_here * length
    tile = (SUBLANES, LANES)
    weights = jnp.transpose(weight, (1, 0, 2))
    norm_params = jnp.zeros((SUBLANES, width), F32).at[0].set(layer_norm_gain).at[1].set(layer_norm_bias)
    x = inputs.reshape(tokens, width)
    u, normed_t, mean, scale = project(x, norm_params, weights)

    starts = jnp.cumsum(doc_lengths, axis=-1) - doc_lengths
    places = jnp.arange(length, dtype=jnp.int32)
    hits = (places[None, :, None] == starts[:, None, :]).astype(F32)
    keep = 1.0 - jnp.sum(hits, axis=-1)
    gate_params = jnp.stack([forget_weight, reset_weight, forget_bias, reset_bias]).reshape((4,) + tile)
    mixed, passed, reset_grad, gate_grads, final_state, sums = recur(
        keep, u.reshape(3, rows_here, length, width), inputs, out_grad, gate_params
    )
    final_state = final_state.reshape(rows_here, width)
    sums = sums.reshape(4, width)

    du = jnp.concatenate([gate_grads.reshape(2, tokens, width), reset_grad.reshape(1, tokens, width)])
    weight_part = jnp.einsum("it,ato->aio", normed_t, du, preferred_element_type=F32).astype(BF16)
    dn = jnp.einsum("ato,aio->ti", du, weights, preferred_element_type=F32)
    me = lax.axis_index("ch")
    mine = lax.dynamic_slice_in_dim(dn, me * width, width, 1)
    theirs = lax.dynamic_slice_in_dim(dn, (1 - me) * width, width, 1).astype(BF16)
    dn = mine + lax.ppermute(theirs, "ch", [(0, 1), (1, 0)]).astype(F32)
    scale = scale[:, :1]
    xhat = (x.astype(F32) - mean[:, :1]) * scale
    gain_part = jnp.sum(dn * xhat, axis=0)
    shift_part = jnp.sum(dn, axis=0)
    dxhat = dn * layer_norm_gain
    first, second = lax.psum((jnp.sum(dxhat, axis=1), jnp.sum(dxhat * xhat, axis=1)), "ch")
    back = scale * (dxhat - first[:, None] / full - xhat * second[:, None] / full)
    input_grad = (back.reshape(rows_here, length, width) + passed.astype(F32)).astype(BF16)
    summed = lax.psum(jnp.concatenate([sums, gain_part[None], shift_part[None]]), "rows")
    weight_grad = lax.psum(weight_part, "rows").astype(F32)
    weight_grad = jnp.transpose(weight_grad, (1, 0, 2))
    return (
        mixed, input_grad, final_state, weight_grad, summed[4], summed[5], summed[0], summed[1], summed[2], summed[3],
    )


def solution(mesh):
    rows_ch = P("rows", None, "ch")
    ch = P("ch")
    in_specs = (rows_ch, P("rows", None), ch, ch, P(None, None, "ch"), ch, ch, ch, ch, rows_ch)
    out_specs = (rows_ch, rows_ch, P("rows", "ch"), P(None, None, "ch"), ch, ch, ch, ch, ch, ch)
    return jax.shard_map(on_device, mesh=mesh, in_specs=in_specs, out_specs=out_specs, check_vma=False)
```

profile of v0, /device:TPU:0, one launch (start us, length us, event | category | flops | bytes accessed | tf_op | source)
XLA Modules:
  0.0 485.6 jit_solution(5589563487686402384)
XLA Ops:
  7.2 0.0 all-reduce.4.cloned.1.call-start
  7.2 0.9 reduce_window_sum.11
  8.1 0.7 sub.34
  8.8 0.1 convert_reduce_fusion
  8.9 0.6 broadcast_subtract_fusion.keep_ref
  9.5 0.7 scatter.6
  10.2 0.8 scatter.9.params_ref
  10.9 0.0 copy-start.3
  10.9 0.6 copy-done.3
  11.6 0.0 copy-start.7
  11.6 0.0 copy-start.8
  11.6 0.0 copy-start.9
  11.6 0.0 copy-start.10
  11.6 101.1 %project.1 = (f32[3,2048,1024]{2,1,0:T(8,128)}, bf16[2048,2048]{1,0:T(8,128)(2,1)}, f32[2048,128]{1,0:T(8,128)}, f32[2048,128]{1,0:T(8,128)}) custom-call(bf16[2048,1024]{1,0:T(8,128)(2,1)} %bitcast.42, f32[8,1024]{1,0:T(8,128)} %copy-done.3, bf16[3,2048,1024]{2,1,0:T(8,128)(2,1)} %bitcast.45), custom_call_target="tpu_custom_call" | custom-call | tf_op jit(solution)/shard_map/project/pallas_call | solution.py:132
  112.7 0.0 copy-done.7
  112.7 0.0 copy-done.8
  112.7 0.0 copy-done.9
  112.7 0.0 copy-done.10
  112.7 0.6 pad_maximum_fusion.6.params_ref
  113.3 39.8 %recur.1 = (bf16[2,1024,1024]{2,1,0:T(8,128)(2,1)}, bf16[2,1024,1024]{2,1,0:T(8,128)(2,1)}, bf16[2,1024,1024]{2,1,0:T(8,128)(2,1)}, bf16[2,2,1024,1024]{3,2,1,0:...) custom-call(f32[2,1024]{1,0:T(2,128)} %broadcast_subtract_fusion.keep_ref, f32[3,2,1024,1024]{3,2,1,0:T(8,128)} %bitcast.44, ...), custom_call_target="tpu_custom_call" | custom-call | tf_op jit(solution)/shard_map/recur/pallas_call | solution.py:300
  153.1 34.6 %convolution_bitcast_fusion = f32[2048,2048]{1,0:T(8,128)} fusion(bf16[1,2048,1024]{2,1,0:T(8,128)(2,1)} %bitcast.66, bf16[2,2048,1024]{2,1,0:T(8,128)(2,1)} %bitcast.64, bf16[2048,3,1024]{2,0,1:T(8,128)(2,1)} %param.18), kind=kOutput, calls=%fused_computation.2 | convolution fusion | flops 25776095232 | bytes 41943040 | tf_op jit(solution)/shard_map/ato,aio->ti/dot_general | solution.py:353
  187.7 0.0 copy-start.11
  187.7 6.3 %dynamic-slice_convert_fusion = bf16[2048,1024]{1,0:T(8,128)(2,1)} fusion(f32[2048,2048]{1,0:T(8,128)} %convolution_bitcast_fusion, s32[]{:T(128)S(6)} %select_n.7), kind=kLoop, calls=%fused_computation.11 | loop fusion | bytes 8388612 | tf_op jit(solution)/shard_map/convert_element_type | solution.py:356
  194.0 1.9 collective-permute-start
  195.9 0.0 copy-done.11
  195.9 30.8 %convert_bitcast_fusion = bf16[2048,3,1024]{0,2,1:T(8,128)(2,1)} fusion(bf16[2048,2048]{1,0:T(8,128)(2,1)S(1)} %copy-done.11, bf16[1,2048,1024]{2,1,0:T(8,128)(2,1)} %bitcast.67, bf16[2,2048,1024]{2,1,0:T(8,128)(2,1)} %bitcast.65), kind=kOutput, calls=%fused_computation.1 | convolution fusion | flops 25782386688 | bytes 33554432 | tf_op jit(solution)/shard_map/it,ato->aio/dot_general | solution.py:352
  226.8 0.0 copy-start.6
  226.8 0.0 copy-start.5
  226.8 0.0 copy-start.1
  226.8 0.0 copy-start.2
  226.8 0.0 copy-start.4
  226.8 0.0 all-reduce.4.cloned.1.call-update
  226.8 0.6 copy-done.6
  227.5 0.6 copy.32
  228.1 0.0 copy-done.5
  228.1 0.0 copy-done.1
  228.1 0.3 copy-done.2
  228.4 0.6 slice_reduce_fusion
  229.0 57.1 %collective-permute-done = bf16[2048,1024]{1,0:T(8,128)(2,1)} collective-permute-done((bf16[2048,1024]{1,0:T(8,128)(2,1)}, bf16[2048,1024]{1,0:T(8,128)(2,1)}, u32[]{:S(2)}, u32[]{:S(2)}) %collective-permute-start) | collective-permute-done | bytes 4194336 | tf_op jit(solution)/shard_map/ppermute | solution.py:357
  286.1 0.0 copy-done.4
  286.1 10.5 %multiply_reduce_fusion = (f32[1024]{0:T(1024)S(1)}, f32[2048]{0:T(1024)S(1)}, f32[2048]{0:T(1024)S(1)}, f32[1024]{0:T(1024)S(1)}, f32[2048,1024]{1,0:T(8,128)}) fusion(f32[2048]{0:T(1024)S(1)} %get-tuple-element.97, f32[2048]{0:T(1024)S(1)} %get-tuple-element.98, bf16[2,1024,1024]{2,1,0:T(8,128)(2,1)} %x_ref.1, f32[1024]{0:T(1024)S(1)} %copy-done.4, ...), kind=kLoop, calls=%fused_computation.5 | loop fusion | flops 25159680 | bytes 25210884 | tf_op jit(solution)/shard_map/reduce_sum | solution.py:360
  296.6 8.0 %all-reduce.1 = (f32[2048]{0:T(1024)S(1)}, f32[2048]{0:T(1024)S(1)}) all-reduce(f32[2048]{0:T(1024)S(1)} %get-tuple-element.85, f32[2048]{0:T(1024)S(1)} %get-tuple-element.86), channel_id=1, replica_groups=mesh['rows'=16,'ch'=2] {'ch'}, use_global_device_ids=true, to_apply=%region_5.6 | all-reduce | flops 4096 | bytes 32768 | tf_op jit(solution)/shard_map/psum | solution.py:363
  304.6 60.1 %psum.31 = f32[6,1024]{1,0:T(8,128)S(1)} all-reduce(f32[6,1024]{1,0:T(8,128)S(1)} %pad_maximum_fusion.5), channel_id=1, replica_groups=mesh['rows'=16,'ch'=2] {'rows'}, use_global_device_ids=true, to_apply=%region_9.10 | all-reduce | flops 6144 | bytes 49152 | tf_op jit(solution)/shard_map/psum | solution.py:366
  364.7 0.6 fusion.7
  365.3 0.0 copy-start
  365.3 6.7 %subtract_multiply_fusion = f32[2048,1024]{1,0:T(8,128)S(1)} fusion(f32[2048,1024]{1,0:T(8,128)} %get-tuple-element.90, f32[2048]{0:T(1024)S(1)} %get-tuple-element.88, f32[2048]{0:T(1024)S(1)} %get-tuple-element.97, f32[2048]{0:T(1024)S(1)} %broadcast_multiply_fusion, f32[1024]{0:T(1024)S(1)} %copy-done.4, f32[2048]{0:T(1024)S(1)} %get-tuple-element.98, ...), kind=kLoop, calls=%fused_computation.7 | loop fusion | flops 18874368 | bytes 21008384 | tf_op jit(solution)/shard_map/mul | solution.py:364
  372.0 0.0 copy-done
  372.0 3.6 add_convert_fusion
  375.6 85.4 %all-reduce.4.cloned.1.call-done = bf16[2048,3,1024]{0,2,1:T(8,128)(2,1)} async-done(((bf16[2048,3,1024]{0,2,1:T(8,128)(2,1)}), bf16[2048,3,1024]{0,2,1:T(8,128)(2,1)}) %all-reduce.4.cloned.1.call-update) | async-done | bytes 12582928 | tf_op jit(solution)/shard_map/psum | solution.py:367
  461.0 17.8 %copy.25 = f32[2048,3,1024]{2,0,1:T(8,128)} copy(bf16[2048,3,1024]{0,2,1:T(8,128)(2,1)} %all-reduce.4.cloned.1.call-done) | data formatting | bytes 37748736
  (3 shorter events, 0.0 us)
Async XLA Ops:
  7.2 453.8 %all-reduce.4.cloned.1.call-start = ((), (), s32[]{:S(2)}) async-start(), calls=%async_computation | async-start | bytes 25165824 | tf_op jit(solution)/shard_map/psum | solution.py:367
  10.9 0.6 copy-start.3
  11.6 101.1 %copy-start.7 = (f32[1024]{0:T(1024)S(1)}, f32[1024]{0:T(1024)}, u32[]{:S(2)}) copy-start(f32[1024]{0:T(1024)} %param.22) | copy-start | bytes 12292
  11.6 101.1 %copy-start.8 = (f32[1024]{0:T(1024)S(1)}, f32[1024]{0:T(1024)}, u32[]{:S(2)}) copy-start(f32[1024]{0:T(1024)} %param.21) | copy-start | bytes 12292
  11.6 101.1 %copy-start.9 = (f32[1024]{0:T(1024)S(1)}, f32[1024]{0:T(1024)}, u32[]{:S(2)}) copy-start(f32[1024]{0:T(1024)} %param.20) | copy-start | bytes 12292
  11.6 101.1 %copy-start.10 = (f32[1024]{0:T(1024)S(1)}, f32[1024]{0:T(1024)}, u32[]{:S(2)}) copy-start(f32[1024]{0:T(1024)} %param.19) | copy-start | bytes 12292
  187.7 8.2 %copy-start.11 = (bf16[2048,2048]{1,0:T(8,128)(2,1)S(1)}, bf16[2048,2048]{1,0:T(8,128)(2,1)}, u32[]{:S(2)}) copy-start(bf16[2048,2048]{1,0:T(8,128)(2,1)} %get-tuple-element.52) | copy-start | bytes 25165828
  194.0 92.1 %collective-permute-start = (bf16[2048,1024]{1,0:T(8,128)(2,1)}, bf16[2048,1024]{1,0:T(8,128)(2,1)}, u32[]{:S(2)}, u32[]{:S(2)}) collective-permute-start(bf16[2048,1024]{1,0:T(8,128)(2,1)} %dynamic-slice_convert_fusion), channel_id=1, source_target_pairs={{0,1},{1,0},{2,3},{3,2},{4,5},{5,4},{6,7},{7,6},{8,9},{9,8},{10,11... | collective-permute-start | bytes 12582920 | tf_op jit(solution)/shard_map/ppermute | solution.py:357
  226.8 0.7 copy-start.6
  226.8 1.3 copy-start.5
  226.8 1.3 copy-start.1
  226.8 1.6 copy-start.2
  226.8 59.3 %copy-start.4 = (f32[1024]{0:T(1024)S(1)}, f32[1024]{0:T(1024)}, u32[]{:S(2)}) copy-start(f32[1024]{0:T(1024)} %param.16) | copy-start | bytes 12292
  365.3 6.7 %copy-start = (bf16[2,1024,1024]{2,1,0:T(8,128)(2,1)S(1)}, bf16[2,1024,1024]{2,1,0:T(8,128)(2,1)}, u32[]{:S(2)}) copy-start(bf16[2,1024,1024]{2,1,0:T(8,128)(2,1)} %get-tuple-element.50) | copy-start | bytes 12582916
Sparse Core Ops, SparseCore 0:
  227.0 233.9 all-reduce.3
where the time goes:
time: 487 us; the launch traced here: 486 us
  waiting for transfers between devices  142 us (29%)
  Pallas kernels  141 us (29%)
  blocking collectives  68.1 us (14%)
  matrix products  65.4 us (13%)
  local copies, waits for them, and re-layouts  28.9 us (6%)
  other arithmetic  23.6 us (5%)
  between operations  14.2 us (3%)
    pallas_call x1, Pallas kernels, project(): pl.pallas_call(project_kernel, out_shape=(jax.ShapeDtypeStruct((3, tokens...  101 us
    psum x1, waiting for transfers between devices, on_device(): weight_grad = lax.psum(weight_part, 'rows').astype(F32)  85.4 us
    psum x1, blocking collectives, on_device(): lax.psum(jnp.concatenate([sums, gain_part[None], shift_part[None]]), 'rows')  60.1 us
    ppermute x1, waiting for transfers between devices, on_device(): dn = mine + lax.ppermute(theirs, 'ch', [(0, 1), (1, 0)]).astype(F32)  57.1 us
    pallas_call x1, Pallas kernels, recur(): pl.pallas_call(recur_kernel, grid=(2 * blocks,), out_shape=(jax.ShapeDtyp...  39.8 us
    dot_general x1, matrix products, on_device(): dn = jnp.einsum('ato,aio->ti', du, weights, preferred_element_type=F32)  34.6 us
    dot_general x1, matrix products, on_device(): jnp.einsum('it,ato->aio', normed_t, du, preferred_element_type=F32)  30.8 us
    unnamed x27, local copies, waits for them, and re-layouts  20 us
  transfers between devices with their start and end apart: 2, of which 2 were waited for; matrix products, arithmetic and copies ran while one was open for 11% of the time, Pallas kernels for 0%

commit v1 on v0

--- a/solution.py
+++ b/solution.py
@@ -324,12 +324,543 @@
     )(keep, u, x, grad, params)
 
 
+JOB_ROWS = 128
+PIECE = 16
+SLAB = 48
+NORM_TOKENS = 256
+RING = 8
+SHORT = 4
+ENDS = 3
+
+
+def finish_kernel(
+    normed_t_ref, gates_ref, reset_ref, weight_ref, x_ref, mean_ref, scale_ref, pass_ref, gain_ref, sums_ref,
+    total_ref, input_grad_ref, small_ref,
+    du, weights, rows_in, mine, core_out, core_in, y_out, y_in, down_out, down_in, up_out, up_in, cross_out, cross_in,
+    ready, dn_all, dn_own, dn_out, dn_in, moment_out, moment_in, x_in, pass_in, mean_in, scale_in, grad_out,
+    norm_sums, small_own, small_in, small_z,
+    load_sem, rows_sem, core_send, core_recv, y_send, y_recv, down_send, down_recv, up_send, up_recv,
+    cross_send, cross_recv, ready_sem, from_low_send, from_low_recv, from_high_send, from_high_recv,
+    pair_send, pair_recv, twin_send, twin_recv, dn_send, dn_recv, moment_send, moment_recv, norm_sem, grad_sem,
+    small_send, small_recv,
+):
+    device = lax.axis_index("rows")
+    devices = lax.axis_size("rows")
+    ch = lax.axis_index("ch")
+    z_stride, y_stride = devices // 4, devices // 8
+    z = device // z_stride
+    y = (device // y_stride) % 2
+    core = device % 2
+    twin = device + 1 - 2 * core
+    pair = device + y_stride * (1 - 2 * y)
+    full, tokens = normed_t_ref.shape
+    width = gates_ref.shape[2]
+    half = full // 2
+    per_gate = half // JOB_ROWS
+    jobs = 3 * per_gate
+    blocks = tokens // NORM_TOKENS
+
+    def aligned(value, size=PIECE):
+        return pl.multiple_of(value, size)
+
+    def place(job, whose):
+        return job // per_gate, aligned(whose * half + (job % per_gate) * JOB_ROWS, JOB_ROWS)
+
+    down_row = aligned(PIECE * y)
+    up_row = aligned(80 - PIECE * y)
+    y_down, y_up = aligned(SLAB * y), aligned(112 - SLAB * y)
+    pair_down, pair_up = aligned(SLAB * (1 - y)), aligned(112 - SLAB * (1 - y))
+
+    def load_du(gate):
+        source = reset_ref if gate == 2 else gates_ref.at[gate]
+        return pltpu.make_async_copy(source, du.at[gate], load_sem.at[gate])
+
+    def load_weight(gate):
+        return pltpu.make_async_copy(weight_ref.at[gate], weights.at[gate], load_sem.at[3 + gate])
+
+    def load_rows(job):
+        slot = job % 2
+        own = aligned(core * half + (job % per_gate) * JOB_ROWS, JOB_ROWS)
+        other = aligned((1 - core) * half + (job % per_gate) * JOB_ROWS, JOB_ROWS)
+        return (
+            pltpu.make_async_copy(
+                normed_t_ref.at[pl.ds(own, JOB_ROWS)], rows_in.at[slot, pl.ds(0, JOB_ROWS)], rows_sem.at[0, slot]
+            ),
+            pltpu.make_async_copy(
+                normed_t_ref.at[pl.ds(other, JOB_ROWS)], rows_in.at[slot, pl.ds(JOB_ROWS, JOB_ROWS)],
+                rows_sem.at[1, slot],
+            ),
+        )
+
+    def remote(source, target, send, recv, where):
+        return pltpu.make_async_remote_copy(
+            src_ref=source, dst_ref=target, send_sem=send, recv_sem=recv, device_id=where, device_id_type=MESH
+        )
+
+    def to_core(job):
+        return remote(
+            core_out.at[job % 2], core_in.at[job % SHORT], core_send.at[job % 2], core_recv.at[job % SHORT],
+            {"rows": twin},
+        )
+
+    def to_y(job):
+        return remote(
+            y_out.at[job % SHORT], y_in.at[job % RING], y_send.at[job % SHORT], y_recv.at[job % RING], {"rows": pair}
+        )
+
+    def to_down(job):
+        return remote(
+            down_out.at[job % SHORT], down_in.at[job % RING], down_send.at[job % SHORT], down_recv.at[job % RING],
+            {"rows": device - z_stride},
+        )
+
+    def to_up(job):
+        return remote(
+            up_out.at[job % SHORT], up_in.at[job % RING], up_send.at[job % SHORT], up_recv.at[job % RING],
+            {"rows": device + z_stride},
+        )
+
+    def to_cross(job):
+        return remote(
+            cross_out.at[job % SHORT], cross_in.at[job % RING], cross_send.at[job % SHORT], cross_recv.at[job % RING],
+            {"rows": pair},
+        )
+
+    def result(job, offset, size, whose):
+        gate, row = place(job, whose)
+        return total_ref.at[gate, pl.ds(aligned(row + offset), size)]
+
+    def keep_ready(job, offset):
+        return pltpu.make_async_copy(
+            ready.at[job % SHORT], result(job, offset, SLAB, core), ready_sem.at[job % SHORT]
+        )
+
+    def gather(job, offset, source, send, recv, where):
+        return remote(source, result(job, offset, SLAB, core), send.at[job % RING], recv.at[job % RING], where)
+
+    def from_low(job, first=False):
+        source = ready.at[job % SHORT] if first else result(job, down_row, SLAB, core)
+        return gather(job, down_row, source, from_low_send, from_low_recv, {"rows": device + z_stride})
+
+    def from_high(job, first=False):
+        source = ready.at[job % SHORT] if first else result(job, up_row, SLAB, core)
+        return gather(job, up_row, source, from_high_send, from_high_recv, {"rows": device - z_stride})
+
+    def to_pair(job):
+        return tuple(
+            remote(
+                result(job, row, PIECE, core), result(job, row, PIECE, core),
+                pair_send.at[side, job % RING], pair_recv.at[side, job % RING], {"rows": pair},
+            )
+            for side, row in enumerate((y_down, y_up))
+        )
+
+    def to_twin(job):
+        return remote(
+            result(job, 0, JOB_ROWS, core), result(job, 0, JOB_ROWS, core),
+            twin_send.at[job % RING], twin_recv.at[job % RING], {"rows": twin},
+        )
+
+    def to_partner(block):
+        return remote(
+            dn_out.at[block % 2], dn_in.at[block % SHORT], dn_send.at[block % 2], dn_recv.at[block % SHORT],
+            {"ch": 1 - ch},
+        )
+
+    def moments(block):
+        return remote(
+            moment_out.at[block % 2], moment_in.at[block % SHORT], moment_send.at[block % 2],
+            moment_recv.at[block % SHORT], {"ch": 1 - ch},
+        )
+
+    def load_norm(block):
+        rows = pl.ds(aligned(block * NORM_TOKENS, NORM_TOKENS), NORM_TOKENS)
+        slot = block % SHORT
+        return tuple(
+            pltpu.make_async_copy(source.at[rows], target.at[slot], norm_sem.at[index, slot])
+            for index, (source, target) in enumerate(
+                ((x_ref, x_in), (pass_ref, pass_in), (mean_ref, mean_in), (scale_ref, scale_in))
+            )
+        )
+
+    def store_grad(block):
+        rows = pl.ds(aligned(block * NORM_TOKENS, NORM_TOKENS), NORM_TOKENS)
+        return pltpu.make_async_copy(grad_out.at[block % 2], input_grad_ref.at[rows], grad_sem.at[block % 2])
+
+    def small_twin():
+        return remote(small_own, small_in.at[0], small_send.at[0], small_recv.at[0], {"rows": twin})
+
+    def small_pair():
+        return remote(small_own, small_in.at[1], small_send.at[1], small_recv.at[1], {"rows": pair})
+
+    def small_column(away):
+        there = (z + away) % 4
+        return remote(
+            small_own, small_z.at[z], small_send.at[1 + away], small_recv.at[1 + away],
+            {"rows": device + (there - z) * z_stride},
+        )
+
+    for gate in range(3):
+        load_du(gate).start()
+        if gate == 0:
+            for copy in load_rows(0):
+                copy.start()
+        load_weight(gate).start()
+
+    barrier = pltpu.get_barrier_semaphore()
+    for where in [{"rows": twin}, {"rows": pair}, {"ch": 1 - ch}] + [
+        {"rows": device + ((z + away) % 4 - z) * z_stride} for away in (1, 2, 3)
+    ]:
+        pl.semaphore_signal(barrier, inc=1, device_id=where, device_id_type=MESH)
+    pl.semaphore_wait(barrier, 6)
+    norm_sums[...] = jnp.zeros_like(norm_sums)
+
+    def is_job(job):
+        return jnp.logical_and(job >= 0, job < jobs)
+
+    def is_block(block):
+        return jnp.logical_and(block >= 0, block < blocks)
+
+    def when(*conditions):
+        return pl.when(functools.reduce(jnp.logical_and, conditions))
+
+    def tick(t, carry):
+        @pl.when(t < 3)
+        def _():
+            for gate in range(3):
+                @pl.when(t == gate)
+                def _():
+                    load_du(gate).wait()
+                    load_weight(gate).wait()
+
+        @when(is_job(t - 2))
+        def _():
+            to_core(t - 2).wait_send()
+
+        @when(is_job(t))
+        def _():
+            gate, slot = t // per_gate, t % 2
+            for copy in load_rows(t):
+                copy.wait()
+
+            @pl.when(t + 1 < jobs)
+            def _():
+                for copy in load_rows(t + 1):
+                    copy.start()
+
+            @pl.loop(0, 2)
+            def _(part):
+                columns = pl.ds(aligned(part * (width // 2), width // 2), width // 2)
+                product = jnp.dot(rows_in[slot], du[gate, :, columns], preferred_element_type=F32)
+                mine[t % RING, :, columns] = product[:JOB_ROWS]
+                core_out[slot, :, columns] = product[JOB_ROWS:].astype(BF16)
+
+            to_core(t).start()
+
+        job = t - 1
+
+        @when(is_job(job))
+        def _():
+            to_core(job).wait_recv()
+            slot = job % RING
+            mine[slot] += core_in[job % SHORT].astype(F32)
+            y_out[job % SHORT, 0:PIECE] = mine[slot, pl.ds(pair_down, PIECE)].astype(BF16)
+            y_out[job % SHORT, PIECE:2 * PIECE] = mine[slot, pl.ds(pair_up, PIECE)].astype(BF16)
+            to_y(job).start()
+
+        @when(is_job(job - 2))
+        def _():
+            to_y(job - 2).wait_send()
+
+        job = t - 2
+
+        @when(is_job(job))
+        def _():
+            to_y(job).wait_recv()
+            slot = job % RING
+            mine[slot, pl.ds(y_down, PIECE)] += y_in[job % RING, 0:PIECE].astype(F32)
+            mine[slot, pl.ds(y_up, PIECE)] += y_in[job % RING, PIECE:2 * PIECE].astype(F32)
+
+        def chain(lag, row, y_place, z_place, hop, arrived, out):
+            job = t - 2 - lag
+
+            @when(is_job(job), lag > 0)
+            def _():
+                hop(job).wait_recv()
+                mine[job % RING, pl.ds(row, SLAB)] += arrived[job % RING].astype(F32)
+
+            @when(is_job(job), lag < ENDS)
+            def _():
+                out[job % SHORT] = mine[job % RING, pl.ds(row, SLAB)].astype(BF16)
+                hop(job).start()
+
+            @when(is_job(job - 2), lag < ENDS)
+            def _():
+                hop(job - 2).wait_send()
+
+            @when(is_job(job), lag == ENDS)
+            def _():
+                ready[job % SHORT, pl.ds(y_place, PIECE)] = mine[
+                    job % RING, pl.ds(aligned(row + y_place), PIECE)
+                ].astype(BF16)
+                cross_out[job % SHORT] = mine[
+                    job % RING, pl.ds(aligned(row + z_place), 2 * PIECE)
+                ].astype(BF16)
+                to_cross(job).start()
+
+            @when(is_job(job - 2), lag == ENDS)
+            def _():
+                to_cross(job - 2).wait_send()
+
+        y_in_down, z_in_down = aligned(2 * PIECE * y), aligned(PIECE * (1 - y))
+        y_in_up, z_in_up = aligned(2 * PIECE * (1 - y)), aligned(PIECE * y)
+        chain(ENDS - z, down_row, y_in_down, z_in_down, to_down, down_in, down_out)
+        chain(z, up_row, y_in_up, z_in_up, to_up, up_in, up_out)
+
+        def spread(lag, row, z_place, hop):
+            job = t - 6 - lag
+
+            @when(is_job(job), lag == 0)
+            def _():
+                to_cross(job).wait_recv()
+                ready[job % SHORT, pl.ds(z_place, 2 * PIECE)] = (
+                    cross_out[job % SHORT].astype(F32) + cross_in[job % RING].astype(F32)
+                ).astype(BF16)
+                keep_ready(job, row).start()
+                hop(job, True).start()
+
+            @when(is_job(job - 2), lag == 0)
+            def _():
+                keep_ready(job - 2, row).wait()
+                hop(job - 2, True).wait_send()
+
+            @when(is_job(job), lag > 0)
+            def _():
+                hop(job).wait_recv()
+
+            @when(is_job(job), lag > 0, lag < ENDS)
+            def _():
+                hop(job).start()
+
+            @when(is_job(job - 2), lag > 0, lag < ENDS)
+            def _():
+                hop(job - 2).wait_send()
+
+        spread(z, down_row, z_in_down, from_low)
+        spread(ENDS - z, up_row, z_in_up, from_high)
+
+        job = t - 9
+
+        @when(is_job(job))
+        def _():
+            for copy in to_pair(job):
+                copy.start()
+
+        @when(is_job(job - 2))
+        def _():
+            for copy in to_pair(job - 2):
+                copy.wait_send()
+
+        job = t - 10
+
+        @when(is_job(job))
+        def _():
+            for copy in to_pair(job):
+                copy.wait_recv()
+            to_twin(job).start()
+
+        @when(is_job(job - 2))
+        def _():
+            to_twin(job - 2).wait_send()
+
+        job = t - 11
+
+        @when(is_job(job))
+        def _():
+            to_twin(job).wait_recv()
+
+        block, gate = t // 3, t % 3
+
+        @when(is_block(block))
+        def _():
+            rows = pl.ds(aligned(block * NORM_TOKENS, NORM_TOKENS), NORM_TOKENS)
+
+            @pl.when(gate == 0)
+            def _():
+                dn_all[...] = jnp.zeros_like(dn_all)
+
+            @pl.loop(0, full // 512)
+            def _(part):
+                columns = pl.ds(aligned(part * 512, 512), 512)
+                dn_all[:, columns] += lax.dot_general(
+                    du[gate, rows, :], weights[gate, columns, :], (((1,), (1,)), ((), ())),
+                    preferred_element_type=F32,
+                )
+
+        own_columns = pl.ds(aligned(ch * width, width), width)
+        other_columns = pl.ds(aligned((1 - ch) * width, width), width)
+
+        @when(is_block(block), gate == 2)
+        def _():
+            dn_out[block % 2] = dn_all[:, other_columns].astype(BF16)
+            dn_own[block % SHORT] = dn_all[:, own_columns]
+            to_partner(block).start()
+            for copy in load_norm(block):
+                copy.start()
+
+        @when(is_block(block - 1), gate == 2)
+        def _():
+            now = block - 1
+            slot = now % SHORT
+            to_partner(now).wait()
+            for copy in load_norm(now):
+                copy.wait()
+
+            def part(index, sums):
+                gain_sum, shift_sum = sums
+                rows = pl.ds(aligned(index * PIECE), PIECE)
+                dn = dn_own[slot, rows, :] + dn_in[slot, rows, :].astype(F32)
+                dn_own[slot, rows, :] = dn
+                scale = scale_in[slot, rows, 0:1]
+                xhat = (x_in[slot, rows, :].astype(F32) - mean_in[slot, rows, 0:1]) * scale
+                gained = dn * xhat
+                dxhat = dn * gain_ref[0:1, :]
+                first = jnp.sum(dxhat, axis=1, keepdims=True)
+                second = jnp.sum(dxhat * xhat, axis=1, keepdims=True)
+                lane = lax.broadcasted_iota(jnp.int32, (PIECE, LANES), 1)
+                moment_out[now % 2, rows, :] = jnp.where(lane < LANES // 2, first, second)
+                return (
+                    gain_sum + gained[:SUBLANES] + gained[SUBLANES:], shift_sum + dn[:SUBLANES] + dn[SUBLANES:],
+                )
+
+            gain_sum, shift_sum = lax.fori_loop(0, NORM_TOKENS // PIECE, part, (norm_sums[0], norm_sums[1]))
+            norm_sums[0] = gain_sum
+            norm_sums[1] = shift_sum
+            moments(now).start()
+
+        @when(is_block(block - 2), gate == 2)
+        def _():
+            now = block - 2
+            slot = now % SHORT
+            moments(now).wait()
+
+            @pl.loop(0, NORM_TOKENS // PIECE)
+            def _(index):
+                rows = pl.ds(aligned(index * PIECE), PIECE)
+                both = (moment_out[now % 2, rows, :] + moment_in[slot, rows, :]) * (1.0 / full)
+                first, second = both[:, 0:1], both[:, LANES // 2:LANES // 2 + 1]
+                scale = scale_in[slot, rows, 0:1]
+                xhat = (x_in[slot, rows, :].astype(F32) - mean_in[slot, rows, 0:1]) * scale
+                back = scale * (dn_own[slot, rows, :] * gain_ref[0:1, :] - first - xhat * second)
+                grad_out[now % 2, rows, :] = (back + pass_in[slot, rows, :].astype(F32)).astype(BF16)
+
+            store_grad(now).start()
+
+        @when(is_block(block - 3), gate == 2)
+        def _():
+            store_grad(block - 3).wait()
+
+        at = 3 * (blocks + 1)
+
+        @pl.when(t == at)
+        def _():
+            small_own[...] = jnp.zeros_like(small_own)
+            small_own[0:4] = sums_ref[...]
+            small_own[4:5] = jnp.sum(norm_sums[0], axis=0, keepdims=True)
+            small_own[5:6] = jnp.sum(norm_sums[1], axis=0, keepdims=True)
+            small_twin().start()
+
+        @pl.when(t == at + 1)
+        def _():
+            small_twin().wait()
+            small_own[...] += small_in[0]
+            small_pair().start()
+
+        @pl.when(t == at + 2)
+        def _():
+            small_pair().wait()
+            small_own[...] += small_in[1]
+            for away in (1, 2, 3):
+                small_column(away).start()
+
+        @pl.when(t == at + 3)
+        def _():
+            for away in (1, 2, 3):
+                small_column(away).wait()
+            small_z[z] = small_own[...]
+            small_ref[...] = (small_z[0] + small_z[1]) + (small_z[2] + small_z[3])
+
+        return carry
+
+    lax.fori_loop(0, jobs + 13, tick, 0)
+
+
+def finish(normed_t, gates, reset, weight, x, mean, scale, passed, gain, sums):
+    full, tokens = normed_t.shape
+    width = x.shape[1]
+    dma = pltpu.SemaphoreType.DMA
+    vmem = pl.BlockSpec(memory_space=pltpu.VMEM)
+    norm = NORM_TOKENS
+    return pl.pallas_call(
+        finish_kernel,
+        out_shape=(
+            jax.ShapeDtypeStruct((3, full, width), BF16),
+            jax.ShapeDtypeStruct((tokens, width), BF16),
+            jax.ShapeDtypeStruct((SUBLANES, width), F32),
+        ),
+        in_specs=[ANY] * 8 + [vmem, vmem],
+        out_specs=(ANY, ANY, vmem),
+        scratch_shapes=[
+            pltpu.VMEM((3, tokens, width), BF16),
+            pltpu.VMEM((3, full, width), BF16),
+            pltpu.VMEM((2, 2 * JOB_ROWS, tokens), BF16),
+            pltpu.VMEM((RING, JOB_ROWS, width), F32),
+            pltpu.VMEM((2, JOB_ROWS, width), BF16),
+            pltpu.VMEM((SHORT, JOB_ROWS, width), BF16),
+            pltpu.VMEM((SHORT, 2 * PIECE, width), BF16),
+            pltpu.VMEM((RING, 2 * PIECE, width), BF16),
+            pltpu.VMEM((SHORT, SLAB, width), BF16),
+            pltpu.VMEM((RING, SLAB, width), BF16),
+            pltpu.VMEM((SHORT, SLAB, width), BF16),
+            pltpu.VMEM((RING, SLAB, width), BF16),
+            pltpu.VMEM((SHORT, 2 * PIECE, width), BF16),
+            pltpu.VMEM((RING, 2 * PIECE, width), BF16),
+            pltpu.VMEM((SHORT, SLAB, width), BF16),
+            pltpu.VMEM((norm, full), F32),
+            pltpu.VMEM((SHORT, norm, width), F32),
+            pltpu.VMEM((2, norm, width), BF16),
+            pltpu.VMEM((SHORT, norm, width), BF16),
+            pltpu.VMEM((2, norm, LANES), F32),
+            pltpu.VMEM((SHORT, norm, LANES), F32),
+            pltpu.VMEM((SHORT, norm, width), BF16),
+            pltpu.VMEM((SHORT, norm, width), BF16),
+            pltpu.VMEM((SHORT, norm, LANES), F32),
+            pltpu.VMEM((SHORT, norm, LANES), F32),
+            pltpu.VMEM((2, norm, width), BF16),
+            pltpu.VMEM((2, SUBLANES, width), F32),
+            pltpu.VMEM((SUBLANES, width), F32),
+            pltpu.VMEM((2, SUBLANES, width), F32),
+            pltpu.VMEM((4, SUBLANES, width), F32),
+            dma((6,)), dma((2, 2)),
+            dma((2,)), dma((SHORT,)), dma((SHORT,)), dma((RING,)), dma((SHORT,)), dma((RING,)),
+            dma((SHORT,)), dma((RING,)), dma((SHORT,)), dma((RING,)), dma((SHORT,)),
+            dma((RING,)), dma((RING,)), dma((RING,)), dma((RING,)),
+            dma((2, RING)), dma((2, RING)), dma((RING,)), dma((RING,)),
+            dma((2,)), dma((SHORT,)), dma((2,)), dma((SHORT,)), dma((4, SHORT)), dma((2,)),
+            dma((5,)), dma((5,)),
+        ],
+        compiler_params=pltpu.CompilerParams(
+            collective_id=1, has_side_effects=True, vmem_limit_bytes=VMEM_LIMIT
+        ),
+        name="finish",
+    )(normed_t, gates, reset, weight, x, mean, scale, passed, gain, sums)
+
+
 def on_device(
     inputs, doc_lengths, layer_norm_gain, layer_norm_bias, weight, forget_weight, reset_weight, forget_bias,
     reset_bias, out_grad,
 ):
     rows_here, length, width = inputs.shape
-    full = width * lax.axis_size("ch")
     tokens = rows_here * length
     tile = (SUBLANES, LANES)
     weights = jnp.transpose(weight, (1, 0, 2))
@@ -345,29 +876,23 @@
     mixed, passed, reset_grad, gate_grads, final_state, sums = recur(
         keep, u.reshape(3, rows_here, length, width), inputs, out_grad, gate_params
     )
-    final_state = final_state.reshape(rows_here, width)
-    sums = sums.reshape(4, width)
-
-    du = jnp.concatenate([gate_grads.reshape(2, tokens, width), reset_grad.reshape(1, tokens, width)])
-    weight_part = jnp.einsum("it,ato->aio", normed_t, du, preferred_element_type=F32).astype(BF16)
-    dn = jnp.einsum("ato,aio->ti", du, weights, preferred_element_type=F32)
-    me = lax.axis_index("ch")
-    mine = lax.dynamic_slice_in_dim(dn, me * width, width, 1)
-    theirs = lax.dynamic_slice_in_dim(dn, (1 - me) * width, width, 1).astype(BF16)
-    dn = mine + lax.ppermute(theirs, "ch", [(0, 1), (1, 0)]).astype(F32)
-    scale = scale[:, :1]
-    xhat = (x.astype(F32) - mean[:, :1]) * scale
-    gain_part = jnp.sum(dn * xhat, axis=0)
-    shift_part = jnp.sum(dn, axis=0)
-    dxhat = dn * layer_norm_gain
-    first, second = lax.psum((jnp.sum(dxhat, axis=1), jnp.sum(dxhat * xhat, axis=1)), "ch")
-    back = scale * (dxhat - first[:, None] / full - xhat * second[:, None] / full)
-    input_grad = (back.reshape(rows_here, length, width) + passed.astype(F32)).astype(BF16)
-    summed = lax.psum(jnp.concatenate([sums, gain_part[None], shift_part[None]]), "rows")
-    weight_grad = lax.psum(weight_part, "rows").astype(F32)
+    weight_grad, input_grad, small = finish(
+        normed_t, gate_grads.reshape(2, tokens, width), reset_grad.reshape(tokens, width), weights, x, mean, scale,
+        passed.reshape(tokens, width), norm_params, sums.reshape(4, width),
+    )
+    weight_grad = weight_grad.astype(F32)
+    devices = lax.axis_size("rows")
+    groups = devices // 16
+    if groups > 1:
+        members = [[] for _ in range(devices // groups)]
+        for device in range(devices):
+            part, core = device // 2, device % 2
+            members[(part // groups) * 2 + core].append(device)
+        weight_grad, small = lax.psum((weight_grad, small), "rows", axis_index_groups=members)
     weight_grad = jnp.transpose(weight_grad, (1, 0, 2))
     return (
-        mixed, input_grad, final_state, weight_grad, summed[4], summed[5], summed[0], summed[1], summed[2], summed[3],
+        mixed, input_grad.reshape(inputs.shape), final_state.reshape(rows_here, width), weight_grad,
+        small[4], small[5], small[0], small[1], small[2], small[3],
     )
 
 

time: 487 us -> 361 us (0.74)
  Pallas kernels: 141 us -> 333 us
  waiting for transfers between devices: 142 us -> 0 us
  blocking collectives: 68.1 us -> 0 us
  matrix products: 65.4 us -> 0 us
  local copies, waits for them, and re-layouts: 28.9 us -> 8.41 us
  between operations: 14.2 us -> 0.68 us
  other arithmetic: 23.6 us -> 18.1 us
    pallas_call x0 -> x1, Pallas kernels: none -> 192 us  [finish(): pl.pallas_call(finish_kernel, out_shape=(jax.ShapeDtypeStruct((3, full, w...]
    psum x1 -> x0, waiting for transfers between devices: 85.4 us -> none  [on_device(): weight_grad = lax.psum(weight_part, 'rows').astype(F32)]
    psum x2 -> x0, blocking collectives: 68.1 us -> none  [the longest x1 60.1 us: on_device(): lax.psum(jnp.concatenate([sums, gain_part[None], shift_part[None]]), 'rows')]
    dot_general x2 -> x0, matrix products: 65.4 us -> none  [the longest x1 34.6 us: on_device(): dn = jnp.einsum('ato,aio->ti', du, weights, preferred_element_type=F32)]
    ppermute x1 -> x0, waiting for transfers between devices: 57.1 us -> none  [on_device(): dn = mine + lax.ppermute(theirs, 'ch', [(0, 1), (1, 0)]).astype(F32)]
    unnamed x27 -> x7, local copies, waits for them, and re-layouts: 20 us -> 5.24 us
    transpose x0 -> x1, other arithmetic: none -> 14.5 us  [on_device(): weight_grad = jnp.transpose(weight_grad, (1, 0, 2))]
    reduce_sum x1 -> x0, other arithmetic: 10.5 us -> none  [on_device(): gain_part = jnp.sum(dn * xhat, axis=0)]
  transfers between devices with their start and end apart: 2 -> 0, of which waited for: 2 -> 0; matrix products, arithmetic and copies ran while one was open for 11% -> 0% of each run, Pallas kernels for 0% -> 0%
where the time goes in v1:
time: 361 us; the launch traced here: 360 us
  Pallas kernels  333 us (92%)
  other arithmetic  18.1 us (5%)
  local copies, waits for them, and re-layouts  8.41 us (2%)
    pallas_call x1, Pallas kernels, finish(): pl.pallas_call(finish_kernel, out_shape=(jax.ShapeDtypeStruct((3, full, w...  192 us
    pallas_call x1, Pallas kernels, project(): pl.pallas_call(project_kernel, out_shape=(jax.ShapeDtypeStruct((3, tokens...  101 us
    pallas_call x1, Pallas kernels, recur(): pl.pallas_call(recur_kernel, grid=(2 * blocks,), out_shape=(jax.ShapeDtyp...  39.9 us
    transpose x1, other arithmetic, on_device(): weight_grad = jnp.transpose(weight_grad, (1, 0, 2))  14.5 us

profile of v1, /device:TPU:0, one launch (start us, length us, event | category | flops | bytes accessed | tf_op | source)
XLA Modules:
  0.0 359.7 jit_solution(16908159729639288672)
XLA Ops:
  0.6 0.9 reduce_window_sum.11
  1.5 0.7 sub.10
  2.2 0.1 convert_reduce_fusion
  2.3 0.6 broadcast_subtract_fusion.keep_ref
  2.9 1.3 pad_maximum_fusion.params_ref
  4.2 0.7 scatter.6
  4.9 0.8 scatter.9.params_ref.gain_ref
  5.7 0.0 copy-start.1
  5.7 0.6 copy-done.1
  6.3 101.0 %project.1 = (f32[3,2048,1024]{2,1,0:T(8,128)}, bf16[2048,2048]{1,0:T(8,128)(2,1)}, f32[2048,128]{1,0:T(8,128)}, f32[2048,128]{1,0:T(8,128)}) custom-call(bf16[2048,1024]{1,0:T(8,128)(2,1)} %bitcast.31, f32[8,1024]{1,0:T(8,128)} %copy-done.1, bf16[3,2048,1024]{2,1,0:T(8,128)(2,1)} %bitcast.29), custom_call_target="tpu_custom_call" | custom-call | tf_op jit(solution)/shard_map/project/pallas_call | solution.py:132
  107.3 39.9 %recur.1 = (bf16[2,1024,1024]{2,1,0:T(8,128)(2,1)}, bf16[2,1024,1024]{2,1,0:T(8,128)(2,1)}, bf16[2,1024,1024]{2,1,0:T(8,128)(2,1)}, bf16[2,2,1024,1024]{3,2,1,0:...) custom-call(f32[2,1024]{1,0:T(2,128)} %broadcast_subtract_fusion.keep_ref, f32[3,2,1024,1024]{3,2,1,0:T(8,128)} %bitcast.33, ...), custom_call_target="tpu_custom_call" | custom-call | tf_op jit(solution)/shard_map/recur/pallas_call | solution.py:300
  147.2 1.3 copy.25
  148.5 1.3 copy.24
  149.8 191.6 %finish.1 = (bf16[3,2048,1024]{2,1,0:T(8,128)(2,1)}, bf16[2048,1024]{1,0:T(8,128)(2,1)}, f32[8,1024]{1,0:T(8,128)}) custom-call(bf16[2048,2048]{1,0:T(8,128)(2,1)} %get-tuple-element.49.normed_t_ref, bf16[2,2048,1024]{2,1,0:T(8,128)(2,1)} %bitcast.34, bf16[2048,1024]{1,0:T(8,128)(2,1)} %bitcast.36, bf16[3,2048,1024]{2,1,0:T(8,128)(2,1)} %bitcast.30, ...), custom_call_target="tpu_custom_call" | custom-call | tf_op jit(solution)/shard_map/finish/pallas_call | solution.py:804
  341.5 1.7 fusion
  343.2 0.0 copy-start
  343.2 14.5 %convert_bitcast_fusion = f32[2048,3,1024]{2,0,1:T(8,128)} fusion(bf16[3,2048,1024]{2,1,0:T(8,128)(2,1)} %get-tuple-element.58), kind=kLoop, calls=%fused_computation | loop fusion | flops 6291456 | bytes 37748736 | tf_op jit(solution)/shard_map/transpose | solution.py:892
  357.7 0.0 copy-done
  357.7 2.0 copy.28
Async XLA Ops:
  5.7 0.6 copy-start.1
  343.2 14.5 %copy-start = (bf16[2048,1024]{1,0:T(8,128)(2,1)S(1)}, bf16[2048,1024]{1,0:T(8,128)(2,1)}, u32[]{:S(2)}) copy-start(bf16[2048,1024]{1,0:T(8,128)(2,1)} %get-tuple-element.56) | copy-start | bytes 12582916

commit v2 on v1

v2 whole, which is shorter than its diff:
```python
import functools

import jax
import jax.numpy as jnp
from jax import lax
from jax.experimental import pallas as pl
from jax.experimental.pallas import tpu as pltpu
from jax.sharding import PartitionSpec as P

MESH = pl.DeviceIdType.MESH
F32 = jnp.float32
BF16 = jnp.bfloat16
EPSILON = 1e-05
LANES = 128
SUBLANES = 8
TILE = (SUBLANES, LANES)
STRETCH = 64
GROUP = 16
ANY = pl.BlockSpec(memory_space=pl.ANY)
IN_VMEM = pl.BlockSpec(memory_space=pltpu.VMEM)
IN_SMEM = pl.BlockSpec(memory_space=pltpu.SMEM)
VMEM_LIMIT = 60 * 1024 * 1024


def aligned(value, size=GROUP):
    return pl.multiple_of(value, size)


def fill_keep(lengths_ref, keep):
    rows_here, length = keep.shape[0], keep.shape[1]
    for row in range(rows_here):
        starts = [jnp.int32(0)]
        for document in range(lengths_ref.shape[1] - 1):
            starts.append(starts[-1] + lengths_ref[row, document])

        @pl.loop(0, length // LANES)
        def _(part):
            place = lax.broadcasted_iota(jnp.int32, (LANES, LANES), 0) + part * LANES
            value = jnp.ones((LANES, LANES), F32)
            for start in starts:
                value = jnp.where(place == start, 0.0, value)
            keep[row, pl.ds(aligned(part * LANES, LANES), LANES), :] = value


def project_kernel(
    lengths_ref, x_ref, gain_ref, shift_ref, weight_ref, grad_ref,
    forget_weight_ref, reset_weight_ref, forget_bias_ref, reset_bias_ref,
    saved_ref, normed_t_ref, mean_ref, scale_ref, mixed_ref, pass_ref, reset_ref, final_ref, sums_ref,
    both, weights, params, keep, normed, normed_t, mean_out, scale_out, u, grad_in, saved, mixed_out, pass_out,
    reset_out, state_s,
    send_sem, recv_sem, own_sem, param_own, param_send, param_recv, weight_sem, grad_sem, out_sem,
):
    ch = lax.axis_index("ch")
    other = 1 - ch
    rows_here, stretches, size, width = x_ref.shape
    full = 2 * width
    tokens = rows_here * size
    own_columns = pl.ds(aligned(ch * width, width), width)

    load_weight = pltpu.make_async_copy(weight_ref, weights, weight_sem)

    def params_of(index, source):
        return (
            pltpu.make_async_copy(source, params.at[ch, index], param_own.at[index]),
            pltpu.make_async_remote_copy(
                src_ref=source, dst_ref=params.at[ch, index], send_sem=param_send.at[index],
                recv_sem=param_recv.at[index], device_id={"ch": other}, device_id_type=MESH,
            ),
        )

    def exchange(stretch):
        return pltpu.make_async_remote_copy(
            src_ref=x_ref.at[:, stretch], dst_ref=both.at[:, stretch, :, own_columns],
            send_sem=send_sem.at[stretch], recv_sem=recv_sem.at[stretch],
            device_id={"ch": other}, device_id_type=MESH,
        )

    def keep_own(stretch):
        return pltpu.make_async_copy(x_ref.at[:, stretch], both.at[:, stretch, :, own_columns], own_sem.at[stretch])

    def load_grad(stretch):
        slot = stretch % 2
        return pltpu.make_async_copy(grad_ref.at[:, stretch], grad_in.at[slot], grad_sem.at[slot])

    def outputs(stretch):
        slot = stretch % 2
        rows = pl.ds(aligned(stretch * tokens, tokens), tokens)
        return tuple(
            pltpu.make_async_copy(source.at[slot], target, out_sem.at[index, slot])
            for index, (source, target) in enumerate((
                (saved, saved_ref.at[stretch]), (normed_t, normed_t_ref.at[:, rows]), (mean_out, mean_ref.at[rows]),
                (scale_out, scale_ref.at[rows]), (mixed_out, mixed_ref.at[:, stretch]), (pass_out, pass_ref.at[rows]),
                (reset_out, reset_ref.at[rows]),
            ))
        )

    load_weight.start()
    load_grad(0).start()
    barrier = pltpu.get_barrier_semaphore()
    pl.semaphore_signal(barrier, inc=1, device_id={"ch": other}, device_id_type=MESH)
    pl.semaphore_wait(barrier, 1)
    for index, source in enumerate((gain_ref, shift_ref)):
        for copy in params_of(index, source):
            copy.start()

    def begin(stretch, carry):
        exchange(stretch).start()
        keep_own(stretch).start()
        return carry

    lax.fori_loop(0, stretches, begin, 0)
    fill_keep(lengths_ref, keep)
    state_s[...] = jnp.zeros_like(state_s)
    sums_ref[...] = jnp.zeros_like(sums_ref)
    for index, source in enumerate((gain_ref, shift_ref)):
        for copy in params_of(index, source):
            copy.wait()
    load_weight.wait()

    def work(stretch, carry):
        slot = stretch % 2
        keep_own(stretch).wait()
        exchange(stretch).wait()
        load_grad(stretch).wait()

        @pl.when(stretch + 1 < stretches)
        def _():
            load_grad(stretch + 1).start()

        @pl.when(stretch >= 2)
        def _():
            for copy in outputs(stretch - 2):
                copy.wait()

        for row in range(rows_here):
            @pl.loop(0, size // GROUP, unroll=2)
            def _(part):
                here = pl.ds(aligned(part * GROUP), GROUP)
                there = pl.ds(aligned(row * size + part * GROUP), GROUP)
                x = both[row, stretch, here, :].astype(F32)
                mean = jnp.sum(x, axis=1, keepdims=True) * (1.0 / full)
                centered = x - mean
                variance = jnp.sum(centered * centered, axis=1, keepdims=True) * (1.0 / full)
                scale = lax.rsqrt(variance + EPSILON)
                gain = jnp.concatenate([params[0, 0], params[1, 0]], axis=1)
                shift = jnp.concatenate([params[0, 1], params[1, 1]], axis=1)
                normed[there, :] = (centered * scale * gain + shift).astype(BF16)
                mean_out[slot, there, :] = jnp.broadcast_to(mean, (GROUP, LANES))
                scale_out[slot, there, :] = jnp.broadcast_to(scale, (GROUP, LANES))

        for gate in range(3):
            u[gate] = jnp.dot(normed[...], weights[gate], preferred_element_type=F32)

        for part in range(full // LANES):
            columns = slice(part * LANES, (part + 1) * LANES)
            normed_t[slot, columns, :] = normed[:, columns].T

        forget_weight = 0.5 * forget_weight_ref[...]
        reset_weight = reset_weight_ref[...]
        half_reset_weight = 0.5 * reset_weight
        forget_bias = 0.5 * forget_bias_ref[...]
        reset_bias = 0.5 * reset_bias_ref[...]

        def group(index, carry):
            state = list(carry[:rows_here])
            weight_sum, bias_sum = carry[rows_here:]
            here = pl.ds(aligned(index * GROUP), GROUP)
            there = [pl.ds(aligned(row * size + index * GROUP), GROUP) for row in range(rows_here)]
            spread = lambda value: value.astype(F32).reshape((GROUP,) + TILE)
            loaded = [
                (
                    spread(u[0, there[row], :]), spread(u[1, there[row], :]), spread(u[2, there[row], :]),
                    spread(both[row, stretch, here, own_columns]), spread(grad_in[slot, row, here, :]),
                )
                for row in range(rows_here)
            ]
            out = [([], [], []) for _ in range(rows_here)]
            for k in range(GROUP):
                time = index * GROUP + k
                for row in range(rows_here):
                    up_x, up_f, up_r, x, grad = (part[k] for part in loaded[row])
                    before = state[row] * keep[row, pl.ds(stretch * size + time, 1), :]
                    bent = jnp.tanh(0.5 * up_f + forget_bias + forget_weight * before)
                    gap = before - up_x
                    after = 0.5 * (before + up_x) + bent * (0.5 * gap)
                    state[row] = after
                    forget = 0.5 * bent + 0.5
                    reset = 0.5 * jnp.tanh(0.5 * up_r + reset_bias + half_reset_weight * before) + 0.5
                    over = after - x
                    direct = grad * reset
                    reset_grad = direct * over * (1.0 - reset)
                    saved[slot, 0, row, time] = direct
                    saved[slot, 1, row, time] = reset_grad * reset_weight
                    saved[slot, 2, row, time] = forget
                    saved[slot, 3, row, time] = gap * forget * (1.0 - forget)
                    saved[slot, 4, row, time] = before
                    weight_sum = weight_sum + reset_grad * before
                    bias_sum = bias_sum + reset_grad
                    out[row][0].append(x + reset * over)
                    out[row][1].append(grad - direct)
                    out[row][2].append(reset_grad)
            flat = lambda parts: jnp.stack(parts).reshape(GROUP, width).astype(BF16)
            for row in range(rows_here):
                mixed_out[slot, row, here, :] = flat(out[row][0])
                pass_out[slot, there[row], :] = flat(out[row][1])
                reset_out[slot, there[row], :] = flat(out[row][2])
            return (*state, weight_sum, bias_sum)

        carried = lax.fori_loop(
            0, size // GROUP, group, (*[state_s[row] for row in range(rows_here)], sums_ref[0], sums_ref[1])
        )
        for row in range(rows_here):
            state_s[row] = carried[row]
        sums_ref[0] = carried[rows_here]
        sums_ref[1] = carried[rows_here + 1]
        for copy in outputs(stretch):
            copy.start()
        return carry

    lax.fori_loop(0, stretches, work, 0)
    for row in range(rows_here):
        final_ref[row:row + 1, :] = state_s[row].reshape(1, width)
    for stretch in (stretches - 2, stretches - 1):
        for copy in outputs(stretch):
            copy.wait()


def project(lengths, x, gain, shift, weight, grad, forget_weight, reset_weight, forget_bias, reset_bias):
    rows_here, stretches, size, width = x.shape
    full = 2 * width
    part = rows_here * size
    tokens = part * stretches
    kept = (5, rows_here, size) + TILE
    dma = pltpu.SemaphoreType.DMA
    shape = jax.ShapeDtypeStruct
    return pl.pallas_call(
        project_kernel,
        out_shape=(
            shape((stretches,) + kept, F32),
            shape((full, tokens), BF16),
            shape((tokens, LANES), F32),
            shape((tokens, LANES), F32),
            shape(x.shape, BF16),
            shape((tokens, width), BF16),
            shape((tokens, width), BF16),
            shape((rows_here, width), F32),
            shape((2,) + TILE, F32),
        ),
        in_specs=[IN_SMEM] + [ANY] * 5 + [IN_VMEM] * 4,
        out_specs=[ANY] * 7 + [IN_VMEM] * 2,
        scratch_shapes=[
            pltpu.VMEM((rows_here, stretches, size, full), BF16),
            pltpu.VMEM((3, full, width), BF16),
            pltpu.VMEM((2, 2, 1, width), F32),
            pltpu.VMEM((rows_here, stretches * size, LANES), F32),
            pltpu.VMEM((part, full), BF16),
            pltpu.VMEM((2, full, part), BF16),
            pltpu.VMEM((2, part, LANES), F32),
            pltpu.VMEM((2, part, LANES), F32),
            pltpu.VMEM((3, part, width), F32),
            pltpu.VMEM((2, rows_here, size, width), BF16),
            pltpu.VMEM((2,) + kept, F32),
            pltpu.VMEM((2, rows_here, size, width), BF16),
            pltpu.VMEM((2, part, width), BF16),
            pltpu.VMEM((2, part, width), BF16),
            pltpu.VMEM((rows_here,) + TILE, F32),
            dma((stretches,)), dma((stretches,)), dma((stretches,)), dma((2,)), dma((2,)), dma((2,)), dma, dma((2,)),
            dma((7, 2)),
        ],
        compiler_params=pltpu.CompilerParams(
            collective_id=0, has_side_effects=True, vmem_limit_bytes=VMEM_LIMIT
        ),
        name="project",
    )(lengths, x, gain, shift, weight, grad, forget_weight, reset_weight, forget_bias, reset_bias)


JOB_ROWS = 128
PIECE = 16
SLAB = 48
NORM_TOKENS = 256
HALF = 32
RING = 8
SHORT = 4
ENDS = 3
SPLIT = 1
UNROLL = 4
HOP = 2
BASE = 1 + HOP
BACK = BASE + (ENDS + 1) * HOP
PAIR = BACK + ENDS * HOP
TWIN = PAIR + HOP
LATE = 3
MINE = BASE + ENDS * HOP + 1
PERIOD = 4
KEPT = 3
AHEAD = 4


def finish_kernel(
    lengths_ref, saved_ref, normed_t_ref, reset_ref, weight_ref, x_ref, mean_ref, scale_ref, pass_ref, gain_ref,
    forget_weight_ref, sums_ref,
    total_ref, input_grad_ref, small_ref,
    du, weights, rows_in, mine, core_out, core_in, y_out, y_in, down_out, down_in, up_out, up_in, cross_out, cross_in,
    ready, dn_own, dn_out, dn_in, moment_out, moment_in, x_in, pass_in, mean_in, scale_in, grad_out,
    norm_sums, keep, saved, state_s, gate_sums, small_own, small_in, small_z,
    load_sem, rows_sem, saved_sem, core_send, core_recv, y_send, y_recv, down_send, down_recv, up_send, up_recv,
    cross_send, cross_recv, ready_sem, from_low_send, from_low_recv, from_high_send, from_high_recv,
    pair_send, pair_recv, twin_send, twin_recv, dn_send, dn_recv, moment_send, moment_recv, norm_sem, grad_sem,
    small_send, small_recv,
):
    device = lax.axis_index("rows")
    devices = lax.axis_size("rows")
    ch = lax.axis_index("ch")
    z_stride, y_stride = devices // 4, devices // 8
    z = device // z_stride
    y = (device // y_stride) % 2
    core = device % 2
    twin = device + 1 - 2 * core
    pair = device + y_stride * (1 - 2 * y)
    full, tokens = normed_t_ref.shape
    rows_here, stretches, size, width = x_ref.shape
    half = full // 2
    narrow = width // SPLIT
    per_part = half // JOB_ROWS
    per_gate = per_part * SPLIT
    jobs = 3 * per_gate
    blocks = tokens // NORM_TOKENS

    def gate_of(job):
        return (job // per_gate + 2) % 3

    def place(job, whose):
        row = aligned(whose * half + (job % per_part) * JOB_ROWS, JOB_ROWS)
        column = aligned(((job // per_part) % SPLIT) * narrow, narrow)
        return gate_of(job), row, column

    down_row = aligned(PIECE * y)
    up_row = aligned(80 - PIECE * y)
    y_down, y_up = aligned(SLAB * y), aligned(112 - SLAB * y)
    pair_down, pair_up = aligned(SLAB * (1 - y)), aligned(112 - SLAB * (1 - y))

    load_reset = pltpu.make_async_copy(reset_ref, du.at[2], load_sem.at[3])

    def load_weight(gate):
        return pltpu.make_async_copy(weight_ref.at[gate], weights.at[gate], load_sem.at[gate])

    def load_rows(job):
        slot = job % 2
        own = aligned(core * half + (job % per_part) * JOB_ROWS, JOB_ROWS)
        other = aligned((1 - core) * half + (job % per_part) * JOB_ROWS, JOB_ROWS)
        return (
            pltpu.make_async_copy(
                normed_t_ref.at[pl.ds(own, JOB_ROWS)], rows_in.at[slot, pl.ds(0, JOB_ROWS)], rows_sem.at[0, slot]
            ),
            pltpu.make_async_copy(
                normed_t_ref.at[pl.ds(other, JOB_ROWS)], rows_in.at[slot, pl.ds(JOB_ROWS, JOB_ROWS)],
                rows_sem.at[1, slot],
            ),
        )

    def remote(source, target, send, recv, where):
        return pltpu.make_async_remote_copy(
            src_ref=source, dst_ref=target, send_sem=send, recv_sem=recv, device_id=where, device_id_type=MESH
        )

    def to_core(job):
        return remote(
            core_out.at[job % 2], core_in.at[job % SHORT], core_send.at[job % 2], core_recv.at[job % SHORT],
            {"rows": twin},
        )

    def to_y(job):
        return remote(
            y_out.at[job % SHORT], y_in.at[job % RING], y_send.at[job % SHORT], y_recv.at[job % RING], {"rows": pair}
        )

    def to_down(job):
        return remote(
            down_out.at[job % SHORT], down_in.at[job % RING], down_send.at[job % SHORT], down_recv.at[job % RING],
            {"rows": device - z_stride},
        )

    def to_up(job):
        return remote(
            up_out.at[job % SHORT], up_in.at[job % RING], up_send.at[job % SHORT], up_recv.at[job % RING],
            {"rows": device + z_stride},
        )

    def to_cross(job):
        return remote(
            cross_out.at[job % SHORT], cross_in.at[job % RING], cross_send.at[job % SHORT], cross_recv.at[job % RING],
            {"rows": pair},
        )

    def result(job, offset, size, whose):
        gate, row, column = place(job, whose)
        return total_ref.at[gate, pl.ds(aligned(row + offset), size), pl.ds(column, narrow)]

    def keep_ready(job, offset):
        return pltpu.make_async_copy(
            ready.at[job % RING], result(job, offset, SLAB, core), ready_sem.at[job % RING]
        )

    def gather(job, offset, source, send, recv, where):
        return remote(source, result(job, offset, SLAB, core), send.at[job % RING], recv.at[job % RING], where)

    def from_low(job, first=False):
        source = ready.at[job % RING] if first else result(job, down_row, SLAB, core)
        return gather(job, down_row, source, from_low_send, from_low_recv, {"rows": device + z_stride})

    def from_high(job, first=False):
        source = ready.at[job % RING] if first else result(job, up_row, SLAB, core)
        return gather(job, up_row, source, from_high_send, from_high_recv, {"rows": device - z_stride})

    def to_pair(job):
        return tuple(
            remote(
                result(job, row, PIECE, core), result(job, row, PIECE, core),
                pair_send.at[side, job % RING], pair_recv.at[side, job % RING], {"rows": pair},
            )
            for side, row in enumerate((y_down, y_up))
        )

    def to_twin(job):
        return remote(
            result(job, 0, JOB_ROWS, core), result(job, 0, JOB_ROWS, core),
            twin_send.at[job % RING], twin_recv.at[job % RING], {"rows": twin},
        )

    def to_partner(block):
        return remote(
            dn_out.at[block % 2], dn_in.at[block % SHORT], dn_send.at[block % 2], dn_recv.at[block % SHORT],
            {"ch": 1 - ch},
        )

    def moments(block):
        return remote(
            moment_out.at[block % 2], moment_in.at[block % SHORT], moment_send.at[block % 2],
            moment_recv.at[block % SHORT], {"ch": 1 - ch},
        )

    pieces = NORM_TOKENS // (rows_here * size)

    def first_row(block):
        return aligned(tokens - NORM_TOKENS * (block + 1), NORM_TOKENS)

    def load_norm(block):
        rows = pl.ds(first_row(block), NORM_TOKENS)
        slot = block % KEPT
        return tuple(
            pltpu.make_async_copy(source.at[rows], target.at[slot], norm_sem.at[index, slot])
            for index, (source, target) in enumerate(((pass_ref, pass_in), (mean_ref, mean_in), (scale_ref, scale_in)))
        ) + tuple(
            pltpu.make_async_copy(
                x_ref.at[:, stretches - pieces * (block + 1) + piece], x_in.at[slot, piece],
                norm_sem.at[3 + piece, slot],
            )
            for piece in range(pieces)
        )

    def store_grad(block):
        return tuple(
            pltpu.make_async_copy(
                grad_out.at[block % 2, piece], input_grad_ref.at[:, stretches - pieces * (block + 1) + piece],
                grad_sem.at[piece, block % 2],
            )
            for piece in range(pieces)
        )

    def load_saved(turn):
        slot = turn % AHEAD
        return pltpu.make_async_copy(
            saved_ref.at[stretches - 1 - turn // 2, :, :, pl.ds(aligned((1 - turn % 2) * HALF, HALF), HALF)],
            saved.at[slot], saved_sem.at[slot],
        )

    def small_twin():
        return remote(small_own, small_in.at[0], small_send.at[0], small_recv.at[0], {"rows": twin})

    def small_pair():
        return remote(small_own, small_in.at[1], small_send.at[1], small_recv.at[1], {"rows": pair})

    def small_column(away):
        there = (z + away) % 4
        return remote(
            small_own, small_z.at[z], small_send.at[1 + away], small_recv.at[1 + away],
            {"rows": device + (there - z) * z_stride},
        )

    load_reset.start()
    for copy in load_rows(0):
        copy.start()
    for turn in range(AHEAD - 1):
        load_saved(turn).start()
    for gate in range(3):
        load_weight(gate).start()

    barrier = pltpu.get_barrier_semaphore()
    for where in [{"rows": twin}, {"rows": pair}, {"ch": 1 - ch}] + [
        {"rows": device + ((z + away) % 4 - z) * z_stride} for away in (1, 2, 3)
    ]:
        pl.semaphore_signal(barrier, inc=1, device_id=where, device_id_type=MESH)
    pl.semaphore_wait(barrier, 6)
    norm_sums[...] = jnp.zeros_like(norm_sums)
    state_s[...] = jnp.zeros_like(state_s)
    gate_sums[...] = jnp.zeros_like(gate_sums)
    fill_keep(lengths_ref, keep)
    turns = 2 * stretches
    turns_tick = turns // per_gate
    load_reset.wait()

    def is_job(job):
        return jnp.logical_and(job >= 0, job < jobs)

    def is_block(block):
        return jnp.logical_and(block >= 0, block < blocks)

    def when(*conditions):
        return pl.when(functools.reduce(jnp.logical_and, conditions))

    def tick(t, carry):
        job = t - 1

        @when(is_job(job))
        def _():
            to_core(job).wait_recv()
            slot = job % MINE
            mine[slot] += core_in[job % SHORT].astype(F32)
            y_out[job % SHORT, 0:PIECE] = mine[slot, pl.ds(pair_down, PIECE)].astype(BF16)
            y_out[job % SHORT, PIECE:2 * PIECE] = mine[slot, pl.ds(pair_up, PIECE)].astype(BF16)
            to_y(job).start()

        @when(is_job(job - LATE))
        def _():
            to_y(job - LATE).wait_send()

        job = t - BASE

        @when(is_job(job))
        def _():
            to_y(job).wait_recv()
            slot = job % MINE
            mine[slot, pl.ds(y_down, PIECE)] += y_in[job % RING, 0:PIECE].astype(F32)
            mine[slot, pl.ds(y_up, PIECE)] += y_in[job % RING, PIECE:2 * PIECE].astype(F32)

        def chain(lag, row, y_place, z_place, hop, arrived, out):
            job = t - BASE - HOP * lag

            @when(is_job(job), lag > 0)
            def _():
                hop(job).wait_recv()
                mine[job % MINE, pl.ds(row, SLAB)] += arrived[job % RING].astype(F32)

            @when(is_job(job), lag < ENDS)
            def _():
                out[job % SHORT] = mine[job % MINE, pl.ds(row, SLAB)].astype(BF16)
                hop(job).start()

            @when(is_job(job - LATE), lag < ENDS)
            def _():
                hop(job - LATE).wait_send()

            @when(is_job(job), lag == ENDS)
            def _():
                ready[job % RING, pl.ds(y_place, PIECE)] = mine[
                    job % MINE, pl.ds(aligned(row + y_place), PIECE)
                ].astype(BF16)
                cross_out[job % SHORT] = mine[
                    job % MINE, pl.ds(aligned(row + z_place), 2 * PIECE)
                ].astype(BF16)
                to_cross(job).start()

            @when(is_job(job - LATE), lag == ENDS)
            def _():
                to_cross(job - LATE).wait_send()

        y_in_down, z_in_down = aligned(2 * PIECE * y), aligned(PIECE * (1 - y))
        y_in_up, z_in_up = aligned(2 * PIECE * (1 - y)), aligned(PIECE * y)
        chain(ENDS - z, down_row, y_in_down, z_in_down, to_down, down_in, down_out)
        chain(z, up_row, y_in_up, z_in_up, to_up, up_in, up_out)

        def spread(lag, row, z_place, hop):
            job = t - BACK - HOP * lag

            @when(is_job(job), lag == 0)
            def _():
                to_cross(job).wait_recv()
                ready[job % RING, pl.ds(z_place, 2 * PIECE)] = (
                    cross_out[job % SHORT].astype(F32) + cross_in[job % RING].astype(F32)
                ).astype(BF16)
                keep_ready(job, row).start()
                hop(job, True).start()

            @when(is_job(job - LATE), lag == 0)
            def _():
                keep_ready(job - LATE, row).wait()
                hop(job - LATE, True).wait_send()

            @when(is_job(job), lag > 0)
            def _():
                hop(job).wait_recv()

            @when(is_job(job), lag > 0, lag < ENDS)
            def _():
                hop(job).start()

            @when(is_job(job - LATE), lag > 0, lag < ENDS)
            def _():
                hop(job - LATE).wait_send()

        spread(z, down_row, z_in_down, from_low)
        spread(ENDS - z, up_row, z_in_up, from_high)

        job = t - PAIR

        @when(is_job(job))
        def _():
            for copy in to_pair(job):
                copy.start()

        @when(is_job(job - LATE))
        def _():
            for copy in to_pair(job - LATE):
                copy.wait_send()

        job = t - TWIN

        @when(is_job(job))
        def _():
            for copy in to_pair(job):
                copy.wait_recv()
            to_twin(job).start()

        @when(is_job(job - LATE))
        def _():
            to_twin(job - LATE).wait_send()

        job = t - TWIN - 1

        @when(is_job(job))
        def _():
            to_twin(job).wait_recv()

        @when(is_job(t - 2))
        def _():
            to_core(t - 2).wait_send()

        @when(is_job(t))
        def _():
            gate, slot = gate_of(t), t % 2
            for copy in load_rows(t):
                copy.wait()

            @pl.when(t + 1 < jobs)
            def _():
                for copy in load_rows(t + 1):
                    copy.start()

            columns = pl.ds(aligned(((t // per_part) % SPLIT) * narrow, narrow), narrow)
            product = jnp.dot(rows_in[slot], du[gate, :, columns], preferred_element_type=F32)
            mine[t % MINE] = product[:JOB_ROWS]
            core_out[slot] = product[JOB_ROWS:].astype(BF16)
            to_core(t).start()

        @pl.when(t < per_gate)
        def _():
            forget_weight = forget_weight_ref[...]

            def back_half(turn, carry):
                load_saved(turn).wait()

                @pl.when(turn + AHEAD - 1 < turns)
                def _():
                    load_saved(turn + AHEAD - 1).start()

                slot = turn % AHEAD
                stretch, start = stretches - 1 - turn // 2, (1 - turn % 2) * HALF

                def group(back, carry):
                    index = HALF // PIECE - 1 - back
                    running = list(carry[:rows_here])
                    weight_sum, bias_sum = carry[rows_here:]
                    out = [([None] * PIECE, [None] * PIECE) for _ in range(rows_here)]
                    for k in range(PIECE - 1, -1, -1):
                        time = index * PIECE + k
                        for row in range(rows_here):
                            direct, extra, forget, slope, before = (saved[slot, kind, row, time] for kind in range(5))
                            kept = keep[row, pl.ds(stretch * size + start + time, 1), :]
                            state_grad = direct + running[row]
                            through = (forget + slope * forget_weight) * kept
                            running[row] = through * state_grad + extra * kept
                            forget_grad = state_grad * slope
                            weight_sum = weight_sum + forget_grad * before
                            bias_sum = bias_sum + forget_grad
                            out[row][0][k] = state_grad - state_grad * forget
                            out[row][1][k] = forget_grad
                    for row in range(rows_here):
                        rows = pl.ds(aligned((stretch * rows_here + row) * size + start + index * PIECE), PIECE)
                        for gate in range(2):
                            du[gate, rows, :] = jnp.stack(out[row][gate]).reshape(PIECE, width).astype(BF16)
                    return (*running, weight_sum, bias_sum)

                return lax.fori_loop(0, HALF // PIECE, group, carry)

            carried = lax.fori_loop(
                t * turns_tick, (t + 1) * turns_tick, back_half,
                (*[state_s[row] for row in range(rows_here)], gate_sums[0], gate_sums[1]),
            )
            for row in range(rows_here):
                state_s[row] = carried[row]
            gate_sums[0] = carried[rows_here]
            gate_sums[1] = carried[rows_here + 1]

        @pl.when(t == 1)
        def _():
            for gate in range(3):
                load_weight(gate).wait()

        block, phase = (t - 1) // (PERIOD * SPLIT), (t - 1) % (PERIOD * SPLIT)
        rows = pl.ds(first_row(block), NORM_TOKENS)

        def split(index):
            each = size // PIECE
            return index // (rows_here * each), (index // each) % rows_here, pl.ds(aligned(index % each * PIECE), PIECE)

        def back(whose, part):
            columns = pl.ds(aligned(whose * width + part * narrow, narrow), narrow)
            return sum(
                lax.dot_general(
                    du[gate, rows, :], weights[gate, columns, :], (((1,), (1,)), ((), ())),
                    preferred_element_type=F32,
                )
                for gate in range(3)
            )

        @when(is_block(block), phase < SPLIT)
        def _():
            columns = pl.ds(aligned(phase * narrow, narrow), narrow)
            dn_out[block % 2, :, columns] = back(1 - ch, phase).astype(BF16)

        @when(is_block(block), phase == SPLIT - 1)
        def _():
            to_partner(block).start()
            for copy in load_norm(block):
                copy.start()

        @when(is_block(block), phase >= SPLIT, phase < 2 * SPLIT)
        def _():
            columns = pl.ds(aligned((phase - SPLIT) * narrow, narrow), narrow)
            dn_own[block % KEPT, :, columns] = back(ch, phase - SPLIT)

        @when(is_block(block - 1), phase == 2 * SPLIT)
        def _():
            now = block - 1
            slot = now % KEPT
            to_partner(now).wait()
            for copy in load_norm(now):
                copy.wait()

            def part(index, sums):
                gain_sum, shift_sum = sums
                rows = pl.ds(aligned(index * PIECE), PIECE)
                piece, row, inner = split(index)
                dn = dn_own[slot, rows, :] + dn_in[now % SHORT, rows, :].astype(F32)
                dn_own[slot, rows, :] = dn
                scale = scale_in[slot, rows, 0:1]
                xhat = (x_in[slot, piece, row, inner, :].astype(F32) - mean_in[slot, rows, 0:1]) * scale
                gained = dn * xhat
                dxhat = dn * gain_ref[0:1, :]
                first = jnp.sum(dxhat, axis=1, keepdims=True)
                second = jnp.sum(dxhat * xhat, axis=1, keepdims=True)
                lane = lax.broadcasted_iota(jnp.int32, (PIECE, LANES), 1)
                moment_out[now % 2, rows, :] = jnp.where(lane < LANES // 2, first, second)
                return (
                    gain_sum + gained[:SUBLANES] + gained[SUBLANES:], shift_sum + dn[:SUBLANES] + dn[SUBLANES:],
                )

            gain_sum, shift_sum = lax.fori_loop(
                0, NORM_TOKENS // PIECE, part, (norm_sums[0], norm_sums[1]), unroll=UNROLL
            )
            norm_sums[0] = gain_sum
            norm_sums[1] = shift_sum
            moments(now).start()

        @when(is_block(block - 2), phase == 3 * SPLIT)
        def _():
            now = block - 2
            slot = now % KEPT
            moments(now).wait()

            @pl.loop(0, NORM_TOKENS // PIECE, unroll=UNROLL)
            def _(index):
                rows = pl.ds(aligned(index * PIECE), PIECE)
                piece, row, inner = split(index)
                both = (moment_out[now % 2, rows, :] + moment_in[now % SHORT, rows, :]) * (1.0 / full)
                first, second = both[:, 0:1], both[:, LANES // 2:LANES // 2 + 1]
                scale = scale_in[slot, rows, 0:1]
                xhat = (x_in[slot, piece, row, inner, :].astype(F32) - mean_in[slot, rows, 0:1]) * scale
                back = scale * (dn_own[slot, rows, :] * gain_ref[0:1, :] - first - xhat * second)
                grad_out[now % 2, piece, row, inner, :] = (back + pass_in[slot, rows, :].astype(F32)).astype(BF16)

            for copy in store_grad(now):
                copy.start()

        @when(is_block(block - 3), phase == 0)
        def _():
            for copy in store_grad(block - 3):
                copy.wait()

        at = PERIOD * SPLIT * (blocks + 1)

        @pl.when(t == at)
        def _():
            small_own[...] = jnp.zeros_like(small_own)
            small_own[0:1] = gate_sums[0].reshape(1, width)
            small_own[1:2] = sums_ref[0].reshape(1, width)
            small_own[2:3] = gate_sums[1].reshape(1, width)
            small_own[3:4] = sums_ref[1].reshape(1, width)
            small_own[4:5] = jnp.sum(norm_sums[0], axis=0, keepdims=True)
            small_own[5:6] = jnp.sum(norm_sums[1], axis=0, keepdims=True)
            small_twin().start()

        @pl.when(t == at + 1)
        def _():
            small_twin().wait()
            small_own[...] += small_in[0]
            small_pair().start()

        @pl.when(t == at + 1 + HOP)
        def _():
            small_pair().wait()
            small_own[...] += small_in[1]
            for away in (1, 2, 3):
                small_column(away).start()

        @pl.when(t == at + 1 + 2 * HOP)
        def _():
            for away in (1, 2, 3):
                small_column(away).wait()
            small_z[z] = small_own[...]
            small_ref[...] = (small_z[0] + small_z[1]) + (small_z[2] + small_z[3])

        return carry

    lax.fori_loop(0, jobs + TWIN + LATE, tick, 0)


def finish(lengths, saved, normed_t, reset, weight, x, mean, scale, passed, gain, forget_weight, sums):
    full, tokens = normed_t.shape
    rows_here, stretches, size, width = x.shape
    dma = pltpu.SemaphoreType.DMA
    vmem = IN_VMEM
    norm = NORM_TOKENS
    narrow = width // SPLIT
    pieces = norm // (rows_here * size)
    return pl.pallas_call(
        finish_kernel,
        out_shape=(
            jax.ShapeDtypeStruct((3, full, width), BF16),
            jax.ShapeDtypeStruct(x.shape, BF16),
            jax.ShapeDtypeStruct((SUBLANES, width), F32),
        ),
        in_specs=[IN_SMEM] + [ANY] * 8 + [vmem] * 3,
        out_specs=(ANY, ANY, vmem),
        scratch_shapes=[
            pltpu.VMEM((3, tokens, width), BF16),
            pltpu.VMEM((3, full, width), BF16),
            pltpu.VMEM((2, 2 * JOB_ROWS, tokens), BF16),
            pltpu.VMEM((MINE, JOB_ROWS, narrow), F32),
            pltpu.VMEM((2, JOB_ROWS, narrow), BF16),
            pltpu.VMEM((SHORT, JOB_ROWS, narrow), BF16),
            pltpu.VMEM((SHORT, 2 * PIECE, narrow), BF16),
            pltpu.VMEM((RING, 2 * PIECE, narrow), BF16),
            pltpu.VMEM((SHORT, SLAB, narrow), BF16),
            pltpu.VMEM((RING, SLAB, narrow), BF16),
            pltpu.VMEM((SHORT, SLAB, narrow), BF16),
            pltpu.VMEM((RING, SLAB, narrow), BF16),
            pltpu.VMEM((SHORT, 2 * PIECE, narrow), BF16),
            pltpu.VMEM((RING, 2 * PIECE, narrow), BF16),
            pltpu.VMEM((RING, SLAB, narrow), BF16),
            pltpu.VMEM((KEPT, norm, width), F32),
            pltpu.VMEM((2, norm, width), BF16),
            pltpu.VMEM((SHORT, norm, width), BF16),
            pltpu.VMEM((2, norm, LANES), F32),
            pltpu.VMEM((SHORT, norm, LANES), F32),
            pltpu.VMEM((KEPT, pieces, rows_here, size, width), BF16),
            pltpu.VMEM((KEPT, norm, width), BF16),
            pltpu.VMEM((KEPT, norm, LANES), F32),
            pltpu.VMEM((KEPT, norm, LANES), F32),
            pltpu.VMEM((2, pieces, rows_here, size, width), BF16),
            pltpu.VMEM((2, SUBLANES, width), F32),
            pltpu.VMEM((rows_here, stretches * size, LANES), F32),
            pltpu.VMEM((AHEAD, 5, rows_here, HALF) + TILE, F32),
            pltpu.VMEM((rows_here,) + TILE, F32),
            pltpu.VMEM((2,) + TILE, F32),
            pltpu.VMEM((SUBLANES, width), F32),
            pltpu.VMEM((2, SUBLANES, width), F32),
            pltpu.VMEM((4, SUBLANES, width), F32),
            dma((4,)), dma((2, 2)), dma((AHEAD,)),
            dma((2,)), dma((SHORT,)), dma((SHORT,)), dma((RING,)), dma((SHORT,)), dma((RING,)),
            dma((SHORT,)), dma((RING,)), dma((SHORT,)), dma((RING,)), dma((RING,)),
            dma((RING,)), dma((RING,)), dma((RING,)), dma((RING,)),
            dma((2, RING)), dma((2, RING)), dma((RING,)), dma((RING,)),
            dma((2,)), dma((SHORT,)), dma((2,)), dma((SHORT,)), dma((3 + pieces, KEPT)), dma((pieces, 2)),
            dma((5,)), dma((5,)),
        ],
        compiler_params=pltpu.CompilerParams(
            collective_id=1, has_side_effects=True, vmem_limit_bytes=VMEM_LIMIT
        ),
        name="finish",
    )(lengths, saved, normed_t, reset, weight, x, mean, scale, passed, gain, forget_weight, sums)


def on_device(
    inputs, doc_lengths, layer_norm_gain, layer_norm_bias, weight, forget_weight, reset_weight, forget_bias,
    reset_bias, out_grad,
):
    rows_here, length, width = inputs.shape
    weights = jnp.transpose(weight, (1, 0, 2))
    stretched = (rows_here, length // STRETCH, STRETCH, width)
    x = inputs.reshape(stretched)
    gain = layer_norm_gain.reshape(1, width)
    vectors = [vector.reshape(TILE) for vector in (forget_weight, reset_weight, forget_bias, reset_bias)]
    saved, normed_t, mean, scale, mixed, passed, reset_grad, final_state, sums = project(
        doc_lengths, x, gain, layer_norm_bias.reshape(1, width), weights, out_grad.reshape(stretched), *vectors
    )
    weight_grad, input_grad, small = finish(
        doc_lengths, saved, normed_t, reset_grad, weights, x, mean, scale, passed, gain, vectors[0], sums
    )
    weight_grad = weight_grad.astype(F32)
    devices = lax.axis_size("rows")
    groups = devices // 16
    if groups > 1:
        members = [[] for _ in range(devices // groups)]
        for device in range(devices):
            part, core = device // 2, device % 2
            members[(part // groups) * 2 + core].append(device)
        weight_grad, small = lax.psum((weight_grad, small), "rows", axis_index_groups=members)
    weight_grad = jnp.transpose(weight_grad, (1, 0, 2))
    return (
        mixed.reshape(inputs.shape), input_grad.reshape(inputs.shape), final_state, weight_grad,
        small[4], small[5], small[0], small[1], small[2], small[3],
    )


def solution(mesh):
    rows_ch = P("rows", None, "ch")
    ch = P("ch")
    in_specs = (rows_ch, P("rows", None), ch, ch, P(None, None, "ch"), ch, ch, ch, ch, rows_ch)
    out_specs = (rows_ch, rows_ch, P("rows", "ch"), P(None, None, "ch"), ch, ch, ch, ch, ch, ch)
    return jax.shard_map(on_device, mesh=mesh, in_specs=in_specs, out_specs=out_specs, check_vma=False)
```

time: 361 us -> 289 us (0.80)
  Pallas kernels: 333 us -> 266 us
    pallas_call x2 -> x1, Pallas kernels: 141 us -> 102 us  [project(): pl.pallas_call(project_kernel, out_shape=(shape((stretches,) + kept, F32)...]
    pallas_call x1, Pallas kernels: 192 us -> 164 us  [finish(): pl.pallas_call(finish_kernel, out_shape=(jax.ShapeDtypeStruct((3, full, w...]
where the time goes in v2:
time: 289 us
  Pallas kernels  266 us (92%)
  other arithmetic  14.5 us (5%)
  local copies, waits for them, and re-layouts  7.92 us (3%)
    pallas_call x1, Pallas kernels, finish(): pl.pallas_call(finish_kernel, out_shape=(jax.ShapeDtypeStruct((3, full, w...  164 us
    pallas_call x1, Pallas kernels, project(): pl.pallas_call(project_kernel, out_shape=(shape((stretches,) + kept, F32)...  102 us
    transpose x1, other arithmetic, on_device(): weight_grad = jnp.transpose(weight_grad, (1, 0, 2))  14.5 us
    unnamed x9, local copies, waits for them, and re-layouts  6.32 us

profile of v2, /device:TPU:0, one launch (start us, length us, event | category | flops | bytes accessed | tf_op | source)
XLA Modules:
  0.0 288.9 jit_solution(4923748076856222185)
XLA Ops:
  0.6 102.2 %project.1 = (f32[16,5,2,64,8,128]{5,4,3,2,1,0:T(8,128)}, bf16[2048,2048]{1,0:T(8,128)(2,1)}, f32[2048,128]{1,0:T(8,128)}, f32[2048,128]{1,0:T(8,128)}, bf16[2,1...) custom-call(s32[2,8]{1,0:T(2,128)} %lengths_ref.3, ...), custom_call_target="tpu_custom_call" | custom-call | tf_op jit(solution)/shard_map/project/pallas_call | solution.py:236
  102.8 163.6 %finish.1 = (bf16[3,2048,1024]{2,1,0:T(8,128)(2,1)}, bf16[2,16,64,1024]{3,2,1,0:T(8,128)(2,1)}, f32[8,1024]{1,0:T(8,128)}) custom-call(s32[2,8]{1,0:T(2,128)} %lengths_ref.3, f32[16,5,2,64,8,128]{5,4,3,2,1,0:T(8,128)} %get-tuple-element.23.saved_ref, bf16[2048,2048]{1,0:T(8,128)(2,1)} %get-tuple-element.24.normed_t_ref, ...), custom_call_target="tpu_custom_call" | custom-call | tf_op jit(solution)/shard_map/finish/pallas_call | solution.py:856
  266.4 1.6 fusion
  268.0 0.0 copy-start
  268.0 14.5 %convert_bitcast_fusion = f32[2048,3,1024]{2,0,1:T(8,128)} fusion(bf16[3,2048,1024]{2,1,0:T(8,128)(2,1)} %get-tuple-element.32), kind=kLoop, calls=%fused_computation | loop fusion | flops 6291456 | bytes 37748736 | tf_op jit(solution)/shard_map/transpose | solution.py:939
  282.5 0.0 copy-done
  282.5 0.0 copy-start.1
  282.6 2.1 copy.23
  284.7 1.6 copy-done.1
  286.3 0.0 copy-start.2
  286.3 2.0 copy.24
  288.3 0.0 copy-done.2
  288.3 0.6 copy.25
Async XLA Ops:
  268.0 14.5 %copy-start = (bf16[2,16,64,1024]{3,2,1,0:T(8,128)(2,1)S(1)}, bf16[2,16,64,1024]{3,2,1,0:T(8,128)(2,1)}, u32[]{:S(2)}) copy-start(bf16[2,16,64,1024]{3,2,1,0:T(8,128)(2,1)} %get-tuple-element.22) | copy-start | bytes 12582916
  282.5 3.7 %copy-start.1 = (bf16[2,16,64,1024]{3,2,1,0:T(8,128)(2,1)S(1)}, bf16[2,16,64,1024]{3,2,1,0:T(8,128)(2,1)}, u32[]{:S(2)}) copy-start(bf16[2,16,64,1024]{3,2,1,0:T(8,128)(2,1)} %get-tuple-element.30) | copy-start | bytes 12582916
  286.3 2.0 copy-start.2

commit v3 on v2

--- a/solution.py
+++ b/solution.py
@@ -45,8 +45,8 @@
 def project_kernel(
     lengths_ref, x_ref, gain_ref, shift_ref, weight_ref, grad_ref,
     forget_weight_ref, reset_weight_ref, forget_bias_ref, reset_bias_ref,
-    saved_ref, normed_t_ref, mean_ref, scale_ref, mixed_ref, pass_ref, reset_ref, final_ref, sums_ref,
-    both, weights, params, keep, normed, normed_t, mean_out, scale_out, u, grad_in, saved, mixed_out, pass_out,
+    saved_ref, forget_ref, normed_t_ref, mean_ref, scale_ref, mixed_ref, pass_ref, reset_ref, final_ref, sums_ref,
+    both, weights, params, keep, normed, normed_t, mean_out, scale_out, u, grad_in, saved, forget_out, mixed_out, pass_out,
     reset_out, state_s,
     send_sem, recv_sem, own_sem, param_own, param_send, param_recv, weight_sem, grad_sem, out_sem,
 ):
@@ -88,7 +88,7 @@
         return tuple(
             pltpu.make_async_copy(source.at[slot], target, out_sem.at[index, slot])
             for index, (source, target) in enumerate((
-                (saved, saved_ref.at[stretch]), (normed_t, normed_t_ref.at[:, rows]), (mean_out, mean_ref.at[rows]),
+                (saved, saved_ref.at[stretch]), (forget_out, forget_ref.at[stretch]), (normed_t, normed_t_ref.at[:, rows]), (mean_out, mean_ref.at[rows]),
                 (scale_out, scale_ref.at[rows]), (mixed_out, mixed_ref.at[:, stretch]), (pass_out, pass_ref.at[rows]),
                 (reset_out, reset_ref.at[rows]),
             ))
@@ -156,8 +156,7 @@
             normed_t[slot, columns, :] = normed[:, columns].T
 
         forget_weight = 0.5 * forget_weight_ref[...]
-        reset_weight = reset_weight_ref[...]
-        half_reset_weight = 0.5 * reset_weight
+        half_reset_weight = 0.5 * reset_weight_ref[...]
         forget_bias = 0.5 * forget_bias_ref[...]
         reset_bias = 0.5 * reset_bias_ref[...]
 
@@ -175,6 +174,7 @@
                 for row in range(rows_here)
             ]
             out = [([], [], []) for _ in range(rows_here)]
+            held = [None] * rows_here
             for k in range(GROUP):
                 time = index * GROUP + k
                 for row in range(rows_here):
@@ -189,11 +189,14 @@
                     over = after - x
                     direct = grad * reset
                     reset_grad = direct * over * (1.0 - reset)
-                    saved[slot, 0, row, time] = direct
-                    saved[slot, 1, row, time] = reset_grad * reset_weight
-                    saved[slot, 2, row, time] = forget
-                    saved[slot, 3, row, time] = gap * forget * (1.0 - forget)
-                    saved[slot, 4, row, time] = before
+                    forget_out[slot, row, time] = forget
+                    kinds = (direct, gap * forget * (1.0 - forget), before)
+                    if k % 2 == 0:
+                        held[row] = kinds
+                    else:
+                        for kind in range(3):
+                            both_steps = jnp.concatenate([held[row][kind], kinds[kind]], axis=0)
+                            saved[slot, kind, row, index * (GROUP // 2) + k // 2] = both_steps.astype(BF16)
                     weight_sum = weight_sum + reset_grad * before
                     bias_sum = bias_sum + reset_grad
                     out[row][0].append(x + reset * over)
@@ -230,13 +233,15 @@
     full = 2 * width
     part = rows_here * size
     tokens = part * stretches
-    kept = (5, rows_here, size) + TILE
+    kept = (3, rows_here, size // 2, 2 * SUBLANES, LANES)
+    kept_forget = (rows_here, size) + TILE
     dma = pltpu.SemaphoreType.DMA
     shape = jax.ShapeDtypeStruct
     return pl.pallas_call(
         project_kernel,
         out_shape=(
-            shape((stretches,) + kept, F32),
+            shape((stretches,) + kept, BF16),
+            shape((stretches,) + kept_forget, F32),
             shape((full, tokens), BF16),
             shape((tokens, LANES), F32),
             shape((tokens, LANES), F32),
@@ -247,7 +252,7 @@
             shape((2,) + TILE, F32),
         ),
         in_specs=[IN_SMEM] + [ANY] * 5 + [IN_VMEM] * 4,
-        out_specs=[ANY] * 7 + [IN_VMEM] * 2,
+        out_specs=[ANY] * 8 + [IN_VMEM] * 2,
         scratch_shapes=[
             pltpu.VMEM((rows_here, stretches, size, full), BF16),
             pltpu.VMEM((3, full, width), BF16),
@@ -259,13 +264,14 @@
             pltpu.VMEM((2, part, LANES), F32),
             pltpu.VMEM((3, part, width), F32),
             pltpu.VMEM((2, rows_here, size, width), BF16),
-            pltpu.VMEM((2,) + kept, F32),
+            pltpu.VMEM((2,) + kept, BF16),
+            pltpu.VMEM((2,) + kept_forget, F32),
             pltpu.VMEM((2, rows_here, size, width), BF16),
             pltpu.VMEM((2, part, width), BF16),
             pltpu.VMEM((2, part, width), BF16),
             pltpu.VMEM((rows_here,) + TILE, F32),
             dma((stretches,)), dma((stretches,)), dma((stretches,)), dma((2,)), dma((2,)), dma((2,)), dma, dma((2,)),
-            dma((7, 2)),
+            dma((8, 2)),
         ],
         compiler_params=pltpu.CompilerParams(
             collective_id=0, has_side_effects=True, vmem_limit_bytes=VMEM_LIMIT
@@ -291,18 +297,21 @@
 TWIN = PAIR + HOP
 LATE = 3
 MINE = BASE + ENDS * HOP + 1
-PERIOD = 4
+PERIOD = 3
+OFFSET = 8
+MEET = 2
+LEAVE = 3
 KEPT = 3
 AHEAD = 4
 
 
 def finish_kernel(
-    lengths_ref, saved_ref, normed_t_ref, reset_ref, weight_ref, x_ref, mean_ref, scale_ref, pass_ref, gain_ref,
-    forget_weight_ref, sums_ref,
+    lengths_ref, saved_ref, forget_ref, normed_t_ref, reset_ref, weight_ref, x_ref, mean_ref, scale_ref, pass_ref, gain_ref,
+    forget_weight_ref, reset_weight_ref, sums_ref,
     total_ref, input_grad_ref, small_ref,
     du, weights, rows_in, mine, core_out, core_in, y_out, y_in, down_out, down_in, up_out, up_in, cross_out, cross_in,
-    ready, dn_own, dn_out, dn_in, moment_out, moment_in, x_in, pass_in, mean_in, scale_in, grad_out,
-    norm_sums, keep, saved, state_s, gate_sums, small_own, small_in, small_z,
+    ready, dn_own, dn_out, dn_in, moment_own, moment_out, moment_in, x_in, pass_in, mean_in, scale_in, grad_out,
+    norm_sums, keep, saved, forgets, state_s, gate_sums, small_own, small_in, small_z,
     load_sem, rows_sem, saved_sem, core_send, core_recv, y_send, y_recv, down_send, down_recv, up_send, up_recv,
     cross_send, cross_recv, ready_sem, from_low_send, from_low_recv, from_high_send, from_high_recv,
     pair_send, pair_recv, twin_send, twin_recv, dn_send, dn_recv, moment_send, moment_recv, norm_sem, grad_sem,
@@ -330,8 +339,8 @@
         return (job // per_gate + 2) % 3
 
     def place(job, whose):
-        row = aligned(whose * half + (job % per_part) * JOB_ROWS, JOB_ROWS)
-        column = aligned(((job // per_part) % SPLIT) * narrow, narrow)
+        row = aligned(whose * half + (job // SPLIT % per_part) * JOB_ROWS, JOB_ROWS)
+        column = aligned((job % SPLIT) * narrow, narrow)
         return gate_of(job), row, column
 
     down_row = aligned(PIECE * y)
@@ -344,10 +353,10 @@
     def load_weight(gate):
         return pltpu.make_async_copy(weight_ref.at[gate], weights.at[gate], load_sem.at[gate])
 
-    def load_rows(job):
-        slot = job % 2
-        own = aligned(core * half + (job % per_part) * JOB_ROWS, JOB_ROWS)
-        other = aligned((1 - core) * half + (job % per_part) * JOB_ROWS, JOB_ROWS)
+    def load_rows(turn):
+        slot = turn % 2
+        own = aligned(core * half + (turn % per_part) * JOB_ROWS, JOB_ROWS)
+        other = aligned((1 - core) * half + (turn % per_part) * JOB_ROWS, JOB_ROWS)
         return (
             pltpu.make_async_copy(
                 normed_t_ref.at[pl.ds(own, JOB_ROWS)], rows_in.at[slot, pl.ds(0, JOB_ROWS)], rows_sem.at[0, slot]
@@ -429,14 +438,14 @@
 
     def to_partner(block):
         return remote(
-            dn_out.at[block % 2], dn_in.at[block % SHORT], dn_send.at[block % 2], dn_recv.at[block % SHORT],
+            dn_out.at[block % KEPT], dn_in.at[block % RING], dn_send.at[block % KEPT], dn_recv.at[block % RING],
             {"ch": 1 - ch},
         )
 
     def moments(block):
         return remote(
-            moment_out.at[block % 2], moment_in.at[block % SHORT], moment_send.at[block % 2],
-            moment_recv.at[block % SHORT], {"ch": 1 - ch},
+            moment_out.at[block % 2], moment_in.at[block % RING], moment_send.at[block % 2],
+            moment_recv.at[block % RING], {"ch": 1 - ch},
         )
 
     pieces = NORM_TOKENS // (rows_here * size)
@@ -468,10 +477,16 @@
         )
 
     def load_saved(turn):
-        slot = turn % AHEAD
-        return pltpu.make_async_copy(
-            saved_ref.at[stretches - 1 - turn // 2, :, :, pl.ds(aligned((1 - turn % 2) * HALF, HALF), HALF)],
-            saved.at[slot], saved_sem.at[slot],
+        slot, stretch, part = turn % AHEAD, stretches - 1 - turn // 2, 1 - turn % 2
+        return (
+            pltpu.make_async_copy(
+                saved_ref.at[stretch, :, :, pl.ds(aligned(part * (HALF // 2), HALF // 2), HALF // 2)],
+                saved.at[slot], saved_sem.at[0, slot],
+            ),
+            pltpu.make_async_copy(
+                forget_ref.at[stretch, :, pl.ds(aligned(part * HALF, HALF), HALF)], forgets.at[slot],
+                saved_sem.at[1, slot],
+            ),
         )
 
     def small_twin():
@@ -491,9 +506,8 @@
     for copy in load_rows(0):
         copy.start()
     for turn in range(AHEAD - 1):
-        load_saved(turn).start()
-    for gate in range(3):
-        load_weight(gate).start()
+        for copy in load_saved(turn):
+            copy.start()
 
     barrier = pltpu.get_barrier_semaphore()
     for where in [{"rows": twin}, {"rows": pair}, {"ch": 1 - ch}] + [
@@ -508,6 +522,8 @@
     turns = 2 * stretches
     turns_tick = turns // per_gate
     load_reset.wait()
+    for gate in range(3):
+        load_weight(gate).start()
 
     def is_job(job):
         return jnp.logical_and(job >= 0, job < jobs)
@@ -647,17 +663,20 @@
 
         @when(is_job(t))
         def _():
-            gate, slot = gate_of(t), t % 2
-            for copy in load_rows(t):
-                copy.wait()
-
-            @pl.when(t + 1 < jobs)
-            def _():
-                for copy in load_rows(t + 1):
+            gate, slot, turn = gate_of(t), t % 2, t // SPLIT
+
+            @pl.when(t % SPLIT == 0)
+            def _():
+                for copy in load_rows(turn):
+                    copy.wait()
+
+            @when(t % SPLIT == 0, t + SPLIT < jobs)
+            def _():
+                for copy in load_rows(turn + 1):
                     copy.start()
 
-            columns = pl.ds(aligned(((t // per_part) % SPLIT) * narrow, narrow), narrow)
-            product = jnp.dot(rows_in[slot], du[gate, :, columns], preferred_element_type=F32)
+            columns = pl.ds(aligned((t % SPLIT) * narrow, narrow), narrow)
+            product = jnp.dot(rows_in[turn % 2], du[gate, :, columns], preferred_element_type=F32)
             mine[t % MINE] = product[:JOB_ROWS]
             core_out[slot] = product[JOB_ROWS:].astype(BF16)
             to_core(t).start()
@@ -665,13 +684,16 @@
         @pl.when(t < per_gate)
         def _():
             forget_weight = forget_weight_ref[...]
+            reset_weight = reset_weight_ref[...]
 
             def back_half(turn, carry):
-                load_saved(turn).wait()
+                for copy in load_saved(turn):
+                    copy.wait()
 
                 @pl.when(turn + AHEAD - 1 < turns)
                 def _():
-                    load_saved(turn + AHEAD - 1).start()
+                    for copy in load_saved(turn + AHEAD - 1):
+                        copy.start()
 
                 slot = turn % AHEAD
                 stretch, start = stretches - 1 - turn // 2, (1 - turn % 2) * HALF
@@ -681,23 +703,35 @@
                     running = list(carry[:rows_here])
                     weight_sum, bias_sum = carry[rows_here:]
                     out = [([None] * PIECE, [None] * PIECE) for _ in range(rows_here)]
+                    rows = [
+                        pl.ds(aligned((stretch * rows_here + row) * size + start + index * PIECE), PIECE)
+                        for row in range(rows_here)
+                    ]
+                    resets = [du[2, rows[row], :].astype(F32).reshape((PIECE,) + TILE) for row in range(rows_here)]
+                    pairs = [None] * rows_here
                     for k in range(PIECE - 1, -1, -1):
                         time = index * PIECE + k
                         for row in range(rows_here):
-                            direct, extra, forget, slope, before = (saved[slot, kind, row, time] for kind in range(5))
+                            if k % 2:
+                                pairs[row] = [
+                                    saved[slot, kind, row, index * (PIECE // 2) + k // 2].astype(F32)
+                                    for kind in range(3)
+                                ]
+                            lanes = slice(SUBLANES, 2 * SUBLANES) if k % 2 else slice(0, SUBLANES)
+                            direct, slope, before = (pair[lanes] for pair in pairs[row])
+                            forget = forgets[slot, row, time]
                             kept = keep[row, pl.ds(stretch * size + start + time, 1), :]
                             state_grad = direct + running[row]
                             through = (forget + slope * forget_weight) * kept
-                            running[row] = through * state_grad + extra * kept
+                            running[row] = through * state_grad + resets[row][k] * reset_weight * kept
                             forget_grad = state_grad * slope
                             weight_sum = weight_sum + forget_grad * before
                             bias_sum = bias_sum + forget_grad
                             out[row][0][k] = state_grad - state_grad * forget
                             out[row][1][k] = forget_grad
                     for row in range(rows_here):
-                        rows = pl.ds(aligned((stretch * rows_here + row) * size + start + index * PIECE), PIECE)
                         for gate in range(2):
-                            du[gate, rows, :] = jnp.stack(out[row][gate]).reshape(PIECE, width).astype(BF16)
+                            du[gate, rows[row], :] = jnp.stack(out[row][gate]).reshape(PIECE, width).astype(BF16)
                     return (*running, weight_sum, bias_sum)
 
                 return lax.fori_loop(0, HALF // PIECE, group, carry)
@@ -711,19 +745,19 @@
             gate_sums[0] = carried[rows_here]
             gate_sums[1] = carried[rows_here + 1]
 
-        @pl.when(t == 1)
+        @pl.when(t == OFFSET)
         def _():
             for gate in range(3):
                 load_weight(gate).wait()
 
-        block, phase = (t - 1) // (PERIOD * SPLIT), (t - 1) % (PERIOD * SPLIT)
-        rows = pl.ds(first_row(block), NORM_TOKENS)
+        block, phase = (t - OFFSET) // PERIOD, (t - OFFSET) % PERIOD
 
         def split(index):
             each = size // PIECE
             return index // (rows_here * each), (index // each) % rows_here, pl.ds(aligned(index % each * PIECE), PIECE)
 
-        def back(whose, part):
+        def back(block, whose, part):
+            rows = pl.ds(first_row(block), NORM_TOKENS)
             columns = pl.ds(aligned(whose * width + part * narrow, narrow), narrow)
             return sum(
                 lax.dot_general(
@@ -736,22 +770,25 @@
         @when(is_block(block), phase < SPLIT)
         def _():
             columns = pl.ds(aligned(phase * narrow, narrow), narrow)
-            dn_out[block % 2, :, columns] = back(1 - ch, phase).astype(BF16)
+            dn_out[block % KEPT, :, columns] = back(block, 1 - ch, phase).astype(BF16)
 
         @when(is_block(block), phase == SPLIT - 1)
         def _():
             to_partner(block).start()
-            for copy in load_norm(block):
+
+        @when(is_block(block - MEET + 1), phase == SPLIT)
+        def _():
+            for copy in load_norm(block - MEET + 1):
                 copy.start()
 
-        @when(is_block(block), phase >= SPLIT, phase < 2 * SPLIT)
+        @when(is_block(block - MEET), phase >= SPLIT, phase < 2 * SPLIT)
         def _():
             columns = pl.ds(aligned((phase - SPLIT) * narrow, narrow), narrow)
-            dn_own[block % KEPT, :, columns] = back(ch, phase - SPLIT)
-
-        @when(is_block(block - 1), phase == 2 * SPLIT)
-        def _():
-            now = block - 1
+            dn_own[(block - MEET) % KEPT, :, columns] = back(block - MEET, ch, phase - SPLIT)
+
+        @when(is_block(block - MEET), phase == 2 * SPLIT)
+        def _():
+            now = block - MEET
             slot = now % KEPT
             to_partner(now).wait()
             for copy in load_norm(now):
@@ -761,7 +798,7 @@
                 gain_sum, shift_sum = sums
                 rows = pl.ds(aligned(index * PIECE), PIECE)
                 piece, row, inner = split(index)
-                dn = dn_own[slot, rows, :] + dn_in[now % SHORT, rows, :].astype(F32)
+                dn = dn_own[slot, rows, :] + dn_in[now % RING, rows, :].astype(F32)
                 dn_own[slot, rows, :] = dn
                 scale = scale_in[slot, rows, 0:1]
                 xhat = (x_in[slot, piece, row, inner, :].astype(F32) - mean_in[slot, rows, 0:1]) * scale
@@ -770,7 +807,7 @@
                 first = jnp.sum(dxhat, axis=1, keepdims=True)
                 second = jnp.sum(dxhat * xhat, axis=1, keepdims=True)
                 lane = lax.broadcasted_iota(jnp.int32, (PIECE, LANES), 1)
-                moment_out[now % 2, rows, :] = jnp.where(lane < LANES // 2, first, second)
+                moment_own[rows, :] = jnp.where(lane == 0, first, second)
                 return (
                     gain_sum + gained[:SUBLANES] + gained[SUBLANES:], shift_sum + dn[:SUBLANES] + dn[SUBLANES:],
                 )
@@ -780,20 +817,24 @@
             )
             norm_sums[0] = gain_sum
             norm_sums[1] = shift_sum
+            for part in range(NORM_TOKENS // LANES):
+                moment_out[now % 2, part] = moment_own[part * LANES:(part + 1) * LANES, :].T[:SUBLANES]
             moments(now).start()
 
-        @when(is_block(block - 2), phase == 3 * SPLIT)
-        def _():
-            now = block - 2
+        @when(is_block(block - LEAVE), phase == PERIOD - 1)
+        def _():
+            now = block - LEAVE
             slot = now % KEPT
             moments(now).wait()
+            for part in range(NORM_TOKENS // LANES):
+                both = (moment_out[now % 2, part] + moment_in[now % RING, part]) * (1.0 / full)
+                moment_own[part * LANES:(part + 1) * LANES, :] = jnp.concatenate([both] * (LANES // SUBLANES), axis=0).T
 
             @pl.loop(0, NORM_TOKENS // PIECE, unroll=UNROLL)
             def _(index):
                 rows = pl.ds(aligned(index * PIECE), PIECE)
                 piece, row, inner = split(index)
-                both = (moment_out[now % 2, rows, :] + moment_in[now % SHORT, rows, :]) * (1.0 / full)
-                first, second = both[:, 0:1], both[:, LANES // 2:LANES // 2 + 1]
+                first, second = moment_own[rows, 0:1], moment_own[rows, 1:2]
                 scale = scale_in[slot, rows, 0:1]
                 xhat = (x_in[slot, piece, row, inner, :].astype(F32) - mean_in[slot, rows, 0:1]) * scale
                 back = scale * (dn_own[slot, rows, :] * gain_ref[0:1, :] - first - xhat * second)
@@ -802,12 +843,12 @@
             for copy in store_grad(now):
                 copy.start()
 
-        @when(is_block(block - 3), phase == 0)
-        def _():
-            for copy in store_grad(block - 3):
+        @when(is_block(block - LEAVE - 1), phase == 0)
+        def _():
+            for copy in store_grad(block - LEAVE - 1):
                 copy.wait()
 
-        at = PERIOD * SPLIT * (blocks + 1)
+        at = OFFSET + PERIOD * (blocks - 1 + MEET) + 2 * SPLIT + 1
 
         @pl.when(t == at)
         def _():
@@ -842,10 +883,17 @@
 
         return carry
 
-    lax.fori_loop(0, jobs + TWIN + LATE, tick, 0)
-
-
-def finish(lengths, saved, normed_t, reset, weight, x, mean, scale, passed, gain, forget_weight, sums):
+    last = max(
+        jobs + TWIN + LATE, OFFSET + PERIOD * (blocks + LEAVE) + 1,
+        OFFSET + PERIOD * (blocks - 1 + MEET) + 2 * SPLIT + 3 + 2 * HOP,
+    )
+    lax.fori_loop(0, last, tick, 0)
+
+
+def finish(
+    lengths, saved, forgets, normed_t, reset, weight, x, mean, scale, passed, gain, forget_weight, reset_weight,
+    sums,
+):
     full, tokens = normed_t.shape
     rows_here, stretches, size, width = x.shape
     dma = pltpu.SemaphoreType.DMA
@@ -860,7 +908,7 @@
             jax.ShapeDtypeStruct(x.shape, BF16),
             jax.ShapeDtypeStruct((SUBLANES, width), F32),
         ),
-        in_specs=[IN_SMEM] + [ANY] * 8 + [vmem] * 3,
+        in_specs=[IN_SMEM] + [ANY] * 9 + [vmem] * 4,
         out_specs=(ANY, ANY, vmem),
         scratch_shapes=[
             pltpu.VMEM((3, tokens, width), BF16),
@@ -879,10 +927,11 @@
             pltpu.VMEM((RING, 2 * PIECE, narrow), BF16),
             pltpu.VMEM((RING, SLAB, narrow), BF16),
             pltpu.VMEM((KEPT, norm, width), F32),
-            pltpu.VMEM((2, norm, width), BF16),
-            pltpu.VMEM((SHORT, norm, width), BF16),
-            pltpu.VMEM((2, norm, LANES), F32),
-            pltpu.VMEM((SHORT, norm, LANES), F32),
+            pltpu.VMEM((KEPT, norm, width), BF16),
+            pltpu.VMEM((RING, norm, width), BF16),
+            pltpu.VMEM((norm, LANES), F32),
+            pltpu.VMEM((2, norm // LANES, SUBLANES, LANES), F32),
+            pltpu.VMEM((RING, norm // LANES, SUBLANES, LANES), F32),
             pltpu.VMEM((KEPT, pieces, rows_here, size, width), BF16),
             pltpu.VMEM((KEPT, norm, width), BF16),
             pltpu.VMEM((KEPT, norm, LANES), F32),
@@ -890,25 +939,71 @@
             pltpu.VMEM((2, pieces, rows_here, size, width), BF16),
             pltpu.VMEM((2, SUBLANES, width), F32),
             pltpu.VMEM((rows_here, stretches * size, LANES), F32),
-            pltpu.VMEM((AHEAD, 5, rows_here, HALF) + TILE, F32),
+            pltpu.VMEM((AHEAD, 3, rows_here, HALF // 2, 2 * SUBLANES, LANES), BF16),
+            pltpu.VMEM((AHEAD, rows_here, HALF) + TILE, F32),
             pltpu.VMEM((rows_here,) + TILE, F32),
             pltpu.VMEM((2,) + TILE, F32),
             pltpu.VMEM((SUBLANES, width), F32),
             pltpu.VMEM((2, SUBLANES, width), F32),
             pltpu.VMEM((4, SUBLANES, width), F32),
-            dma((4,)), dma((2, 2)), dma((AHEAD,)),
+            dma((4,)), dma((2, 2)), dma((2, AHEAD)),
             dma((2,)), dma((SHORT,)), dma((SHORT,)), dma((RING,)), dma((SHORT,)), dma((RING,)),
             dma((SHORT,)), dma((RING,)), dma((SHORT,)), dma((RING,)), dma((RING,)),
             dma((RING,)), dma((RING,)), dma((RING,)), dma((RING,)),
             dma((2, RING)), dma((2, RING)), dma((RING,)), dma((RING,)),
-            dma((2,)), dma((SHORT,)), dma((2,)), dma((SHORT,)), dma((3 + pieces, KEPT)), dma((pieces, 2)),
+            dma((KEPT,)), dma((RING,)), dma((2,)), dma((RING,)), dma((3 + pieces, KEPT)), dma((pieces, 2)),
             dma((5,)), dma((5,)),
         ],
         compiler_params=pltpu.CompilerParams(
             collective_id=1, has_side_effects=True, vmem_limit_bytes=VMEM_LIMIT
         ),
         name="finish",
-    )(lengths, saved, normed_t, reset, weight, x, mean, scale, passed, gain, forget_weight, sums)
+    )(
+        lengths, saved, forgets, normed_t, reset, weight, x, mean, scale, passed, gain, forget_weight, reset_weight, sums
+    )
+
+
+COLLECT_STEPS = 8
+
+
+def collect_kernel(
+    total_ref, mixed_ref, input_grad_ref, final_ref, small_ref,
+    weight_grad_ref, mixed_out, input_grad_out, final_out, gain_out, shift_out, forget_weight_out, reset_weight_out,
+    forget_bias_out, reset_bias_out,
+):
+    weight_grad_ref[...] = total_ref[...].astype(F32)
+    mixed_out[...] = mixed_ref[...]
+    input_grad_out[...] = input_grad_ref[...]
+
+    @pl.when(pl.program_id(0) == 0)
+    def _():
+        final_out[...] = final_ref[...]
+        outs = (forget_weight_out, reset_weight_out, forget_bias_out, reset_bias_out, gain_out, shift_out)
+        for index, out in enumerate(outs):
+            out[...] = small_ref[index:index + 1, :].reshape(TILE)
+
+
+def collect(total, mixed, input_grad, final_state, small):
+    gates, full, width = total.shape
+    total = total.reshape(gates * full, width)
+    mixed, input_grad = (array.reshape(-1, width) for array in (mixed, input_grad))
+    arrays = (total, mixed, input_grad)
+    blocks = [pl.BlockSpec((array.shape[0] // COLLECT_STEPS, width), lambda i: (i, 0)) for array in arrays]
+    whole = lambda *shape: pl.BlockSpec(shape, lambda i: (0,) * len(shape))
+    shape = jax.ShapeDtypeStruct
+    weight_grad, *others = pl.pallas_call(
+        collect_kernel,
+        grid=(COLLECT_STEPS,),
+        out_shape=(
+            shape(total.shape, F32), shape(mixed.shape, BF16), shape(input_grad.shape, BF16),
+            shape(final_state.shape, F32),
+        ) + (shape(TILE, F32),) * 6,
+        in_specs=blocks + [whole(*final_state.shape), whole(*small.shape)],
+        out_specs=blocks + [whole(*final_state.shape)] + [whole(*TILE)] * 6,
+        compiler_params=pltpu.CompilerParams(vmem_limit_bytes=VMEM_LIMIT),
+        name="collect",
+    )(total, mixed, input_grad, final_state, small)
+    return weight_grad.reshape(gates, full, width), *others
 
 
 def on_device(
@@ -921,13 +1016,14 @@
     x = inputs.reshape(stretched)
     gain = layer_norm_gain.reshape(1, width)
     vectors = [vector.reshape(TILE) for vector in (forget_weight, reset_weight, forget_bias, reset_bias)]
-    saved, normed_t, mean, scale, mixed, passed, reset_grad, final_state, sums = project(
+    saved, forgets, normed_t, mean, scale, mixed, passed, reset_grad, final_state, sums = project(
         doc_lengths, x, gain, layer_norm_bias.reshape(1, width), weights, out_grad.reshape(stretched), *vectors
     )
     weight_grad, input_grad, small = finish(
-        doc_lengths, saved, normed_t, reset_grad, weights, x, mean, scale, passed, gain, vectors[0], sums
+        doc_lengths, saved, forgets, normed_t, reset_grad, weights, x, mean, scale, passed, gain, vectors[0],
+        vectors[1], sums,
     )
-    weight_grad = weight_grad.astype(F32)
+    weight_grad, mixed, input_grad, final_state, *vectors = collect(weight_grad, mixed, input_grad, final_state, small)
     devices = lax.axis_size("rows")
     groups = devices // 16
     if groups > 1:
@@ -935,11 +1031,11 @@
         for device in range(devices):
             part, core = device // 2, device % 2
             members[(part // groups) * 2 + core].append(device)
-        weight_grad, small = lax.psum((weight_grad, small), "rows", axis_index_groups=members)
+        weight_grad, vectors = lax.psum((weight_grad, vectors), "rows", axis_index_groups=members)
     weight_grad = jnp.transpose(weight_grad, (1, 0, 2))
     return (
         mixed.reshape(inputs.shape), input_grad.reshape(inputs.shape), final_state, weight_grad,
-        small[4], small[5], small[0], small[1], small[2], small[3],
+        *[vector.reshape(width) for vector in vectors],
     )
 
 

time: 289 us -> 277 us (0.958)
  other arithmetic: 14.5 us -> 0 us
  Pallas kernels: 266 us -> 276 us
  local copies, waits for them, and re-layouts: 7.92 us -> 0 us
    pallas_call x1 -> x2, Pallas kernels: 102 us -> 121 us  [the longest x1 102 us: project(): pl.pallas_call(project_kernel, out_shape=(shape((stretches,) + kept, BF16...]
    transpose x1 -> x0, other arithmetic: 14.5 us -> none  [on_device(): weight_grad = jnp.transpose(weight_grad, (1, 0, 2))]
    pallas_call x1, Pallas kernels: 164 us -> 154 us  [finish(): pl.pallas_call(finish_kernel, out_shape=(jax.ShapeDtypeStruct((3, full, w...]
    unnamed x9 -> x0, local copies, waits for them, and re-layouts: 6.32 us -> none
where the time goes in v3:
time: 277 us
  Pallas kernels  276 us (100%)
    pallas_call x1, Pallas kernels, finish(): pl.pallas_call(finish_kernel, out_shape=(jax.ShapeDtypeStruct((3, full, w...  154 us
    pallas_call x1, Pallas kernels, project(): pl.pallas_call(project_kernel, out_shape=(shape((stretches,) + kept, BF16...  102 us
    pallas_call x1, Pallas kernels, collect(): pl.pallas_call(collect_kernel, grid=(COLLECT_STEPS,), out_shape=(shape(to...  19.6 us

profile of v3, /device:TPU:0, one launch (start us, length us, event | category | flops | bytes accessed | tf_op | source)
XLA Modules:
  0.0 276.5 jit_solution(12528707651858340921)
XLA Ops:
  0.6 101.8 %project.1 = (bf16[16,3,2,32,16,128]{5,4,3,2,1,0:T(8,128)(2,1)}, f32[16,2,64,8,128]{4,3,2,1,0:T(8,128)}, bf16[2048,2048]{1,0:T(8,128)(2,1)}, f32[2048,128]{1,0:T...) custom-call(s32[2,8]{1,0:T(2,128)} %lengths_ref.3, ...), custom_call_target="tpu_custom_call" | custom-call | tf_op jit(solution)/shard_map/project/pallas_call | solution.py:240
  102.5 154.4 %finish.1 = (bf16[3,2048,1024]{2,1,0:T(8,128)(2,1)}, bf16[2,16,64,1024]{3,2,1,0:T(8,128)(2,1)}, f32[8,1024]{1,0:T(8,128)}) custom-call(s32[2,8]{1,0:T(2,128)} %lengths_ref.3, bf16[16,3,2,32,16,128]{5,4,3,2,1,0:T(8,128)(2,1)} %get-tuple-element.33.saved_ref, f32[16,2,64,8,128]{4,3,2,1,0:T(8,128)} %get-tuple-element.34.forget_ref, ...), custom_call_target="tpu_custom_call" | custom-call | tf_op jit(solution)/shard_map/finish/pallas_call | solution.py:904
  256.9 19.6 %collect.1 = (f32[6144,1024]{1,0:T(8,128)}, bf16[2048,1024]{1,0:T(8,128)(2,1)}, bf16[2048,1024]{1,0:T(8,128)(2,1)}, f32[2,1024]{1,0:T(2,128)}, f32[8,128]{1,0:T(...) custom-call(bf16[6144,1024]{1,0:T(8,128)(2,1)} %bitcast.27, ...), custom_call_target="tpu_custom_call" | custom-call | tf_op jit(solution)/shard_map/collect/pallas_call | solution.py:994

commit v4 on v3

--- a/solution.py
+++ b/solution.py
@@ -282,25 +282,27 @@
 
 JOB_ROWS = 128
 PIECE = 16
-SLAB = 48
+QUARTER = 32
 NORM_TOKENS = 256
 HALF = 32
 RING = 8
+LONG = 12
 SHORT = 4
-ENDS = 3
 SPLIT = 1
 UNROLL = 4
 HOP = 2
-BASE = 1 + HOP
-BACK = BASE + (ENDS + 1) * HOP
-PAIR = BACK + ENDS * HOP
-TWIN = PAIR + HOP
+CORE = 1
+AT_Y = CORE + HOP
+AT_MIDDLE = AT_Y + HOP
+AT_READY = AT_MIDDLE + HOP
+AT_GATHER = AT_READY + HOP
+AT_TWIN = AT_GATHER + HOP
+MINE = AT_MIDDLE + 1
 LATE = 3
-MINE = BASE + ENDS * HOP + 1
 PERIOD = 3
-OFFSET = 8
-MEET = 2
-LEAVE = 3
+OFFSET = 4
+MEET = 1
+LEAVE = 2
 KEPT = 3
 AHEAD = 4
 
@@ -309,12 +311,14 @@
     lengths_ref, saved_ref, forget_ref, normed_t_ref, reset_ref, weight_ref, x_ref, mean_ref, scale_ref, pass_ref, gain_ref,
     forget_weight_ref, reset_weight_ref, sums_ref,
     total_ref, input_grad_ref, small_ref,
-    du, weights, rows_in, mine, core_out, core_in, y_out, y_in, down_out, down_in, up_out, up_in, cross_out, cross_in,
+    du, weights, rows_in, mine, core_out, core_in, y_out, y_in, slab_out, slab_in, side_out, side_in, half_out, half_in,
+    swap_out, swap_in, cross_out, cross_in,
     ready, dn_own, dn_out, dn_in, moment_own, moment_out, moment_in, x_in, pass_in, mean_in, scale_in, grad_out,
     norm_sums, keep, saved, forgets, state_s, gate_sums, small_own, small_in, small_z,
-    load_sem, rows_sem, saved_sem, core_send, core_recv, y_send, y_recv, down_send, down_recv, up_send, up_recv,
-    cross_send, cross_recv, ready_sem, from_low_send, from_low_recv, from_high_send, from_high_recv,
-    pair_send, pair_recv, twin_send, twin_recv, dn_send, dn_recv, moment_send, moment_recv, norm_sem, grad_sem,
+    load_sem, rows_sem, saved_sem, core_send, core_recv, y_send, y_recv, slab_send, slab_recv, side_send, side_recv,
+    half_send, half_recv, swap_send, swap_recv, cross_send, cross_recv, ready_sem,
+    gather_send, gather_recv, over_send, over_recv, last_send, last_recv, pair_send, pair_recv, twin_send, twin_recv,
+    dn_send, dn_recv, moment_send, moment_recv, norm_sem, grad_sem,
     small_send, small_recv,
 ):
     device = lax.axis_index("rows")
@@ -343,10 +347,12 @@
         column = aligned((job % SPLIT) * narrow, narrow)
         return gate_of(job), row, column
 
-    down_row = aligned(PIECE * y)
-    up_row = aligned(80 - PIECE * y)
-    y_down, y_up = aligned(SLAB * y), aligned(112 - SLAB * y)
-    pair_down, pair_up = aligned(SLAB * (1 - y)), aligned(112 - SLAB * (1 - y))
+    outer = jnp.logical_or(z == 0, z == 3)
+    inner = jnp.logical_not(outer)
+    inward = device + z_stride * (1 - 2 * (z // 2))
+    outward = device - z_stride * (1 - 2 * (z // 2))
+    y_row, pair_row = aligned(3 * QUARTER * y, QUARTER), aligned(3 * QUARTER * (1 - y), QUARTER)
+    own_half, other_half = aligned(QUARTER * (1 + z // 2), QUARTER), aligned(QUARTER * (2 - z // 2), QUARTER)
 
     load_reset = pltpu.make_async_copy(reset_ref, du.at[2], load_sem.at[3])
 
@@ -383,57 +389,70 @@
             y_out.at[job % SHORT], y_in.at[job % RING], y_send.at[job % SHORT], y_recv.at[job % RING], {"rows": pair}
         )
 
-    def to_down(job):
+    def ring(source, target, send, recv, job, where, size=RING):
         return remote(
-            down_out.at[job % SHORT], down_in.at[job % RING], down_send.at[job % SHORT], down_recv.at[job % RING],
-            {"rows": device - z_stride},
-        )
-
-    def to_up(job):
-        return remote(
-            up_out.at[job % SHORT], up_in.at[job % RING], up_send.at[job % SHORT], up_recv.at[job % RING],
-            {"rows": device + z_stride},
-        )
+            source.at[job % SHORT], target.at[job % size], send.at[job % SHORT], recv.at[job % size], {"rows": where}
+        )
+
+    def to_slab(job):
+        return ring(slab_out, slab_in, slab_send, slab_recv, job, inward, LONG)
+
+    def to_side(job):
+        return ring(side_out, side_in, side_send, side_recv, job, inward, LONG)
+
+    def to_half(job):
+        return ring(half_out, half_in, half_send, half_recv, job, inward)
+
+    def to_swap(job):
+        return ring(swap_out, swap_in, swap_send, swap_recv, job, inward)
 
     def to_cross(job):
-        return remote(
-            cross_out.at[job % SHORT], cross_in.at[job % RING], cross_send.at[job % SHORT], cross_recv.at[job % RING],
-            {"rows": pair},
-        )
+        return ring(cross_out, cross_in, cross_send, cross_recv, job, pair)
 
     def result(job, offset, size, whose):
         gate, row, column = place(job, whose)
         return total_ref.at[gate, pl.ds(aligned(row + offset), size), pl.ds(column, narrow)]
 
-    def keep_ready(job, offset):
-        return pltpu.make_async_copy(
-            ready.at[job % RING], result(job, offset, SLAB, core), ready_sem.at[job % RING]
-        )
-
-    def gather(job, offset, source, send, recv, where):
-        return remote(source, result(job, offset, SLAB, core), send.at[job % RING], recv.at[job % RING], where)
-
-    def from_low(job, first=False):
-        source = ready.at[job % RING] if first else result(job, down_row, SLAB, core)
-        return gather(job, down_row, source, from_low_send, from_low_recv, {"rows": device + z_stride})
-
-    def from_high(job, first=False):
-        source = ready.at[job % RING] if first else result(job, up_row, SLAB, core)
-        return gather(job, up_row, source, from_high_send, from_high_recv, {"rows": device - z_stride})
-
-    def to_pair(job):
+    def keep_ready(job):
+        return tuple(
+            pltpu.make_async_copy(
+                ready.at[job % SHORT, kind], result(job, row, QUARTER, core), ready_sem.at[kind, job % SHORT]
+            )
+            for kind, row in enumerate((y_row, own_half))
+        )
+
+    def gather(job):
         return tuple(
             remote(
-                result(job, row, PIECE, core), result(job, row, PIECE, core),
-                pair_send.at[side, job % RING], pair_recv.at[side, job % RING], {"rows": pair},
+                ready.at[job % SHORT, kind], result(job, row, QUARTER, core), gather_send.at[kind, job % LONG],
+                gather_recv.at[kind, job % LONG], {"rows": outward},
             )
-            for side, row in enumerate((y_down, y_up))
+            for kind, row in enumerate((y_row, own_half))
+        )
+
+    def over(job):
+        return remote(
+            ready.at[job % SHORT, 1], result(job, own_half, QUARTER, core), over_send.at[job % LONG],
+            over_recv.at[job % LONG], {"rows": inward},
+        )
+
+    def last_half(job):
+        return remote(
+            result(job, other_half, QUARTER, core), result(job, other_half, QUARTER, core), last_send.at[job % LONG],
+            last_recv.at[job % LONG], {"rows": outward},
+        )
+
+    def to_pair(job, first=False):
+        source = ready.at[job % SHORT, 0] if first else result(job, y_row, QUARTER, core)
+        return remote(
+            source, result(job, y_row, QUARTER, core), pair_send.at[job % LONG], pair_recv.at[job % LONG],
+            {"rows": pair},
         )
 
     def to_twin(job):
         return remote(
             result(job, 0, JOB_ROWS, core), result(job, 0, JOB_ROWS, core),
-            twin_send.at[job % RING], twin_recv.at[job % RING], {"rows": twin},
+            twin_send.at[job % LONG], twin_recv.at[job % LONG], {"rows": twin},
         )
 
     def to_partner(block):
@@ -509,12 +528,38 @@
         for copy in load_saved(turn):
             copy.start()
 
+    def is_job(job):
+        return jnp.logical_and(job >= 0, job < jobs)
+
+    def is_block(block):
+        return jnp.logical_and(block >= 0, block < blocks)
+
+    def when(*conditions):
+        return pl.when(functools.reduce(jnp.logical_and, conditions))
+
+    def multiply(t):
+        gate, slot, turn = gate_of(t), t % 2, t // SPLIT
+
+        @pl.when(t % SPLIT == 0)
+        def _():
+            for copy in load_rows(turn):
+                copy.wait()
+
+        @when(t % SPLIT == 0, t + SPLIT < jobs)
+        def _():
+            for copy in load_rows(turn + 1):
+                copy.start()
+
+        columns = pl.ds(aligned((t % SPLIT) * narrow, narrow), narrow)
+        product = jnp.dot(rows_in[turn % 2], du[gate, :, columns], preferred_element_type=F32)
+        mine[t % MINE] = product[:JOB_ROWS]
+        core_out[slot] = product[JOB_ROWS:].astype(BF16)
+
     barrier = pltpu.get_barrier_semaphore()
     for where in [{"rows": twin}, {"rows": pair}, {"ch": 1 - ch}] + [
         {"rows": device + ((z + away) % 4 - z) * z_stride} for away in (1, 2, 3)
     ]:
         pl.semaphore_signal(barrier, inc=1, device_id=where, device_id_type=MESH)
-    pl.semaphore_wait(barrier, 6)
     norm_sums[...] = jnp.zeros_like(norm_sums)
     state_s[...] = jnp.zeros_like(state_s)
     gate_sums[...] = jnp.zeros_like(gate_sums)
@@ -525,160 +570,157 @@
     for gate in range(3):
         load_weight(gate).start()
 
-    def is_job(job):
-        return jnp.logical_and(job >= 0, job < jobs)
-
-    def is_block(block):
-        return jnp.logical_and(block >= 0, block < blocks)
-
-    def when(*conditions):
-        return pl.when(functools.reduce(jnp.logical_and, conditions))
+    multiply(0)
+    pl.semaphore_wait(barrier, 6)
 
     def tick(t, carry):
-        job = t - 1
+        job = t - AT_TWIN - 1
+
+        @when(is_job(job))
+        def _():
+            to_twin(job).wait_recv()
+
+        job = t - AT_TWIN
+
+        @when(is_job(job), outer)
+        def _():
+            last_half(job).wait_recv()
+
+        @when(is_job(job))
+        def _():
+            to_pair(job).wait_recv()
+            to_twin(job).start()
+
+        @when(is_job(job - LATE))
+        def _():
+            to_twin(job - LATE).wait_send()
+
+        job = t - AT_GATHER
+
+        @when(is_job(job), outer)
+        def _():
+            for copy in gather(job):
+                copy.wait_recv()
+            to_pair(job).start()
+
+        @when(is_job(job), inner)
+        def _():
+            over(job).wait_recv()
+            last_half(job).start()
+
+        @when(is_job(job - LATE), outer)
+        def _():
+            to_pair(job - LATE).wait_send()
+
+        @when(is_job(job - LATE), inner)
+        def _():
+            last_half(job - LATE).wait_send()
+
+        job = t - AT_READY
+
+        @when(is_job(job), inner)
+        def _():
+            slot = job % SHORT
+            to_swap(job).wait_recv()
+            ready[slot, 0] = (swap_out[slot].astype(F32) + swap_in[job % RING].astype(F32)).astype(BF16)
+            to_cross(job).wait_recv()
+            ready[slot, 1] = (cross_out[slot].astype(F32) + cross_in[job % RING].astype(F32)).astype(BF16)
+            over(job).start()
+            for copy in gather(job):
+                copy.start()
+            to_pair(job, True).start()
+            for copy in keep_ready(job):
+                copy.start()
+
+        @when(is_job(job - LATE), inner)
+        def _():
+            over(job - LATE).wait_send()
+            for copy in gather(job - LATE):
+                copy.wait_send()
+            to_pair(job - LATE, True).wait_send()
+            for copy in keep_ready(job - LATE):
+                copy.wait()
+
+        job = t - AT_MIDDLE
+
+        @when(is_job(job), inner)
+        def _():
+            slot = job % MINE
+            to_half(job).wait_recv()
+            mine[slot, pl.ds(own_half, QUARTER)] += half_in[job % RING].astype(F32)
+            cross_out[job % SHORT] = mine[slot, pl.ds(own_half, QUARTER)].astype(BF16)
+            to_cross(job).start()
+            to_side(job).wait_recv()
+            mine[slot, pl.ds(y_row, QUARTER)] += side_in[job % LONG].astype(F32)
+            swap_out[job % SHORT] = mine[slot, pl.ds(y_row, QUARTER)].astype(BF16)
+            to_swap(job).start()
+
+        @when(is_job(job - LATE), inner)
+        def _():
+            to_cross(job - LATE).wait_send()
+            to_swap(job - LATE).wait_send()
+
+        job = t - AT_Y
+
+        @when(is_job(job))
+        def _():
+            to_y(job).wait_recv()
+            mine[job % MINE, pl.ds(y_row, QUARTER)] += y_in[job % RING].astype(F32)
+
+        @when(is_job(job), outer)
+        def _():
+            side_out[job % SHORT] = mine[job % MINE, pl.ds(y_row, QUARTER)].astype(BF16)
+            to_side(job).start()
+
+        @when(is_job(job), inner)
+        def _():
+            slot = job % MINE
+            to_slab(job).wait_recv()
+            mine[slot, QUARTER:3 * QUARTER] += slab_in[job % LONG].astype(F32)
+            half_out[job % SHORT] = mine[slot, pl.ds(other_half, QUARTER)].astype(BF16)
+            to_half(job).start()
+
+        @when(is_job(job - LATE), outer)
+        def _():
+            to_side(job - LATE).wait_send()
+
+        @when(is_job(job - LATE), inner)
+        def _():
+            to_half(job - LATE).wait_send()
+
+        job = t - CORE
 
         @when(is_job(job))
         def _():
             to_core(job).wait_recv()
             slot = job % MINE
             mine[slot] += core_in[job % SHORT].astype(F32)
-            y_out[job % SHORT, 0:PIECE] = mine[slot, pl.ds(pair_down, PIECE)].astype(BF16)
-            y_out[job % SHORT, PIECE:2 * PIECE] = mine[slot, pl.ds(pair_up, PIECE)].astype(BF16)
+            y_out[job % SHORT] = mine[slot, pl.ds(pair_row, QUARTER)].astype(BF16)
             to_y(job).start()
 
+        @when(is_job(job), outer)
+        def _():
+            slab_out[job % SHORT] = mine[job % MINE, QUARTER:3 * QUARTER].astype(BF16)
+            to_slab(job).start()
+
         @when(is_job(job - LATE))
         def _():
             to_y(job - LATE).wait_send()
 
-        job = t - BASE
-
-        @when(is_job(job))
-        def _():
-            to_y(job).wait_recv()
-            slot = job % MINE
-            mine[slot, pl.ds(y_down, PIECE)] += y_in[job % RING, 0:PIECE].astype(F32)
-            mine[slot, pl.ds(y_up, PIECE)] += y_in[job % RING, PIECE:2 * PIECE].astype(F32)
-
-        def chain(lag, row, y_place, z_place, hop, arrived, out):
-            job = t - BASE - HOP * lag
-
-            @when(is_job(job), lag > 0)
-            def _():
-                hop(job).wait_recv()
-                mine[job % MINE, pl.ds(row, SLAB)] += arrived[job % RING].astype(F32)
-
-            @when(is_job(job), lag < ENDS)
-            def _():
-                out[job % SHORT] = mine[job % MINE, pl.ds(row, SLAB)].astype(BF16)
-                hop(job).start()
-
-            @when(is_job(job - LATE), lag < ENDS)
-            def _():
-                hop(job - LATE).wait_send()
-
-            @when(is_job(job), lag == ENDS)
-            def _():
-                ready[job % RING, pl.ds(y_place, PIECE)] = mine[
-                    job % MINE, pl.ds(aligned(row + y_place), PIECE)
-                ].astype(BF16)
-                cross_out[job % SHORT] = mine[
-                    job % MINE, pl.ds(aligned(row + z_place), 2 * PIECE)
-                ].astype(BF16)
-                to_cross(job).start()
-
-            @when(is_job(job - LATE), lag == ENDS)
-            def _():
-                to_cross(job - LATE).wait_send()
-
-        y_in_down, z_in_down = aligned(2 * PIECE * y), aligned(PIECE * (1 - y))
-        y_in_up, z_in_up = aligned(2 * PIECE * (1 - y)), aligned(PIECE * y)
-        chain(ENDS - z, down_row, y_in_down, z_in_down, to_down, down_in, down_out)
-        chain(z, up_row, y_in_up, z_in_up, to_up, up_in, up_out)
-
-        def spread(lag, row, z_place, hop):
-            job = t - BACK - HOP * lag
-
-            @when(is_job(job), lag == 0)
-            def _():
-                to_cross(job).wait_recv()
-                ready[job % RING, pl.ds(z_place, 2 * PIECE)] = (
-                    cross_out[job % SHORT].astype(F32) + cross_in[job % RING].astype(F32)
-                ).astype(BF16)
-                keep_ready(job, row).start()
-                hop(job, True).start()
-
-            @when(is_job(job - LATE), lag == 0)
-            def _():
-                keep_ready(job - LATE, row).wait()
-                hop(job - LATE, True).wait_send()
-
-            @when(is_job(job), lag > 0)
-            def _():
-                hop(job).wait_recv()
-
-            @when(is_job(job), lag > 0, lag < ENDS)
-            def _():
-                hop(job).start()
-
-            @when(is_job(job - LATE), lag > 0, lag < ENDS)
-            def _():
-                hop(job - LATE).wait_send()
-
-        spread(z, down_row, z_in_down, from_low)
-        spread(ENDS - z, up_row, z_in_up, from_high)
-
-        job = t - PAIR
-
-        @when(is_job(job))
-        def _():
-            for copy in to_pair(job):
-                copy.start()
-
-        @when(is_job(job - LATE))
-        def _():
-            for copy in to_pair(job - LATE):
-                copy.wait_send()
-
-        job = t - TWIN
-
-        @when(is_job(job))
-        def _():
-            for copy in to_pair(job):
-                copy.wait_recv()
-            to_twin(job).start()
-
-        @when(is_job(job - LATE))
-        def _():
-            to_twin(job - LATE).wait_send()
-
-        job = t - TWIN - 1
-
-        @when(is_job(job))
-        def _():
-            to_twin(job).wait_recv()
+        @when(is_job(job - LATE), outer)
+        def _():
+            to_slab(job - LATE).wait_send()
 
         @when(is_job(t - 2))
         def _():
             to_core(t - 2).wait_send()
 
+        @when(t > 0, is_job(t))
+        def _():
+            multiply(t)
+
         @when(is_job(t))
         def _():
-            gate, slot, turn = gate_of(t), t % 2, t // SPLIT
-
-            @pl.when(t % SPLIT == 0)
-            def _():
-                for copy in load_rows(turn):
-                    copy.wait()
-
-            @when(t % SPLIT == 0, t + SPLIT < jobs)
-            def _():
-                for copy in load_rows(turn + 1):
-                    copy.start()
-
-            columns = pl.ds(aligned((t % SPLIT) * narrow, narrow), narrow)
-            product = jnp.dot(rows_in[turn % 2], du[gate, :, columns], preferred_element_type=F32)
-            mine[t % MINE] = product[:JOB_ROWS]
-            core_out[slot] = product[JOB_ROWS:].astype(BF16)
             to_core(t).start()
 
         @pl.when(t < per_gate)
@@ -884,7 +926,7 @@
         return carry
 
     last = max(
-        jobs + TWIN + LATE, OFFSET + PERIOD * (blocks + LEAVE) + 1,
+        jobs + AT_TWIN + LATE, OFFSET + PERIOD * (blocks + LEAVE) + 1,
         OFFSET + PERIOD * (blocks - 1 + MEET) + 2 * SPLIT + 3 + 2 * HOP,
     )
     lax.fori_loop(0, last, tick, 0)
@@ -917,15 +959,19 @@
             pltpu.VMEM((MINE, JOB_ROWS, narrow), F32),
             pltpu.VMEM((2, JOB_ROWS, narrow), BF16),
             pltpu.VMEM((SHORT, JOB_ROWS, narrow), BF16),
-            pltpu.VMEM((SHORT, 2 * PIECE, narrow), BF16),
-            pltpu.VMEM((RING, 2 * PIECE, narrow), BF16),
-            pltpu.VMEM((SHORT, SLAB, narrow), BF16),
-            pltpu.VMEM((RING, SLAB, narrow), BF16),
-            pltpu.VMEM((SHORT, SLAB, narrow), BF16),
-            pltpu.VMEM((RING, SLAB, narrow), BF16),
-            pltpu.VMEM((SHORT, 2 * PIECE, narrow), BF16),
-            pltpu.VMEM((RING, 2 * PIECE, narrow), BF16),
-            pltpu.VMEM((RING, SLAB, narrow), BF16),
+            pltpu.VMEM((SHORT, QUARTER, narrow), BF16),
+            pltpu.VMEM((RING, QUARTER, narrow), BF16),
+            pltpu.VMEM((SHORT, 2 * QUARTER, narrow), BF16),
+            pltpu.VMEM((LONG, 2 * QUARTER, narrow), BF16),
+            pltpu.VMEM((SHORT, QUARTER, narrow), BF16),
+            pltpu.VMEM((LONG, QUARTER, narrow), BF16),
+            pltpu.VMEM((SHORT, QUARTER, narrow), BF16),
+            pltpu.VMEM((RING, QUARTER, narrow), BF16),
+            pltpu.VMEM((SHORT, QUARTER, narrow), BF16),
+            pltpu.VMEM((RING, QUARTER, narrow), BF16),
+            pltpu.VMEM((SHORT, QUARTER, narrow), BF16),
+            pltpu.VMEM((RING, QUARTER, narrow), BF16),
+            pltpu.VMEM((SHORT, 2, QUARTER, narrow), BF16),
             pltpu.VMEM((KEPT, norm, width), F32),
             pltpu.VMEM((KEPT, norm, width), BF16),
             pltpu.VMEM((RING, norm, width), BF16),
@@ -947,10 +993,11 @@
             pltpu.VMEM((2, SUBLANES, width), F32),
             pltpu.VMEM((4, SUBLANES, width), F32),
             dma((4,)), dma((2, 2)), dma((2, AHEAD)),
-            dma((2,)), dma((SHORT,)), dma((SHORT,)), dma((RING,)), dma((SHORT,)), dma((RING,)),
-            dma((SHORT,)), dma((RING,)), dma((SHORT,)), dma((RING,)), dma((RING,)),
-            dma((RING,)), dma((RING,)), dma((RING,)), dma((RING,)),
-            dma((2, RING)), dma((2, RING)), dma((RING,)), dma((RING,)),
+            dma((2,)), dma((SHORT,)), dma((SHORT,)), dma((RING,)), dma((SHORT,)), dma((LONG,)),
+            dma((SHORT,)), dma((LONG,)), dma((SHORT,)), dma((RING,)), dma((SHORT,)), dma((RING,)),
+            dma((SHORT,)), dma((RING,)), dma((2, SHORT)),
+            dma((2, LONG)), dma((2, LONG)), dma((LONG,)), dma((LONG,)), dma((LONG,)), dma((LONG,)),
+            dma((LONG,)), dma((LONG,)), dma((LONG,)), dma((LONG,)),
             dma((KEPT,)), dma((RING,)), dma((2,)), dma((RING,)), dma((3 + pieces, KEPT)), dma((pieces, 2)),
             dma((5,)), dma((5,)),
         ],

time: 277 us -> 270 us (0.975)
  Pallas kernels: 276 us -> 269 us
    pallas_call x1, Pallas kernels: 154 us -> 148 us  [finish(): pl.pallas_call(finish_kernel, out_shape=(jax.ShapeDtypeStruct((3, full, w...]
where the time goes in v4:
time: 270 us
  Pallas kernels  269 us (100%)
    pallas_call x1, Pallas kernels, finish(): pl.pallas_call(finish_kernel, out_shape=(jax.ShapeDtypeStruct((3, full, w...  148 us
    pallas_call x1, Pallas kernels, project(): pl.pallas_call(project_kernel, out_shape=(shape((stretches,) + kept, BF16...  102 us
    pallas_call x1, Pallas kernels, collect(): pl.pallas_call(collect_kernel, grid=(COLLECT_STEPS,), out_shape=(shape(to...  19.6 us

profile of v4, /device:TPU:0, one launch (start us, length us, event | category | flops | bytes accessed | tf_op | source)
XLA Modules:
  0.0 269.8 jit_solution(11717963135386212542)
XLA Ops:
  0.6 101.8 %project.1 = (bf16[16,3,2,32,16,128]{5,4,3,2,1,0:T(8,128)(2,1)}, f32[16,2,64,8,128]{4,3,2,1,0:T(8,128)}, bf16[2048,2048]{1,0:T(8,128)(2,1)}, f32[2048,128]{1,0:T...) custom-call(s32[2,8]{1,0:T(2,128)} %lengths_ref.3, ...), custom_call_target="tpu_custom_call" | custom-call | tf_op jit(solution)/shard_map/project/pallas_call | solution.py:240
  102.5 147.7 %finish.1 = (bf16[3,2048,1024]{2,1,0:T(8,128)(2,1)}, bf16[2,16,64,1024]{3,2,1,0:T(8,128)(2,1)}, f32[8,1024]{1,0:T(8,128)}) custom-call(s32[2,8]{1,0:T(2,128)} %lengths_ref.3, bf16[16,3,2,32,16,128]{5,4,3,2,1,0:T(8,128)(2,1)} %get-tuple-element.33.saved_ref, f32[16,2,64,8,128]{4,3,2,1,0:T(8,128)} %get-tuple-element.34.forget_ref, ...), custom_call_target="tpu_custom_call" | custom-call | tf_op jit(solution)/shard_map/finish/pallas_call | solution.py:946
  250.1 19.6 %collect.1 = (f32[6144,1024]{1,0:T(8,128)}, bf16[2048,1024]{1,0:T(8,128)(2,1)}, bf16[2048,1024]{1,0:T(8,128)(2,1)}, f32[2,1024]{1,0:T(2,128)}, f32[8,128]{1,0:T(...) custom-call(bf16[6144,1024]{1,0:T(8,128)(2,1)} %bitcast.27, ...), custom_call_target="tpu_custom_call" | custom-call | tf_op jit(solution)/shard_map/collect/pallas_call | solution.py:1041

commit v5 on v4

--- a/solution.py
+++ b/solution.py
@@ -17,7 +17,6 @@
 STRETCH = 64
 GROUP = 16
 ANY = pl.BlockSpec(memory_space=pl.ANY)
-IN_VMEM = pl.BlockSpec(memory_space=pltpu.VMEM)
 IN_SMEM = pl.BlockSpec(memory_space=pltpu.SMEM)
 VMEM_LIMIT = 60 * 1024 * 1024
 
@@ -44,11 +43,11 @@
 
 def project_kernel(
     lengths_ref, x_ref, gain_ref, shift_ref, weight_ref, grad_ref,
-    forget_weight_ref, reset_weight_ref, forget_bias_ref, reset_bias_ref,
-    saved_ref, forget_ref, normed_t_ref, mean_ref, scale_ref, mixed_ref, pass_ref, reset_ref, final_ref, sums_ref,
+    forget_weight_in, reset_weight_in, forget_bias_in, reset_bias_in,
+    saved_ref, forget_ref, normed_t_ref, mean_ref, scale_ref, mixed_ref, pass_ref, reset_ref, final_out, sums_out,
     both, weights, params, keep, normed, normed_t, mean_out, scale_out, u, grad_in, saved, forget_out, mixed_out, pass_out,
-    reset_out, state_s,
-    send_sem, recv_sem, own_sem, param_own, param_send, param_recv, weight_sem, grad_sem, out_sem,
+    reset_out, state_s, vectors, final_ref, sums_ref,
+    send_sem, recv_sem, own_sem, param_own, param_send, param_recv, weight_sem, grad_sem, out_sem, small_sem,
 ):
     ch = lax.axis_index("ch")
     other = 1 - ch
@@ -94,8 +93,14 @@
             ))
         )
 
+    loads = [
+        pltpu.make_async_copy(source, vectors.at[index], small_sem.at[index])
+        for index, source in enumerate((forget_weight_in, reset_weight_in, forget_bias_in, reset_bias_in))
+    ]
     load_weight.start()
     load_grad(0).start()
+    for copy in loads:
+        copy.start()
     barrier = pltpu.get_barrier_semaphore()
     pl.semaphore_signal(barrier, inc=1, device_id={"ch": other}, device_id_type=MESH)
     pl.semaphore_wait(barrier, 1)
@@ -115,6 +120,8 @@
     for index, source in enumerate((gain_ref, shift_ref)):
         for copy in params_of(index, source):
             copy.wait()
+    for copy in loads:
+        copy.wait()
     load_weight.wait()
 
     def work(stretch, carry):
@@ -133,7 +140,7 @@
                 copy.wait()
 
         for row in range(rows_here):
-            @pl.loop(0, size // GROUP, unroll=2)
+            @pl.loop(0, size // GROUP, unroll=4)
             def _(part):
                 here = pl.ds(aligned(part * GROUP), GROUP)
                 there = pl.ds(aligned(row * size + part * GROUP), GROUP)
@@ -155,10 +162,7 @@
             columns = slice(part * LANES, (part + 1) * LANES)
             normed_t[slot, columns, :] = normed[:, columns].T
 
-        forget_weight = 0.5 * forget_weight_ref[...]
-        half_reset_weight = 0.5 * reset_weight_ref[...]
-        forget_bias = 0.5 * forget_bias_ref[...]
-        reset_bias = 0.5 * reset_bias_ref[...]
+        forget_weight, half_reset_weight, forget_bias, reset_bias = (0.5 * vectors[index] for index in range(4))
 
         def group(index, carry):
             state = list(carry[:rows_here])
@@ -223,9 +227,17 @@
     lax.fori_loop(0, stretches, work, 0)
     for row in range(rows_here):
         final_ref[row:row + 1, :] = state_s[row].reshape(1, width)
+    stores = [
+        pltpu.make_async_copy(final_ref, final_out, small_sem.at[4]),
+        pltpu.make_async_copy(sums_ref, sums_out, small_sem.at[5]),
+    ]
+    for copy in stores:
+        copy.start()
     for stretch in (stretches - 2, stretches - 1):
         for copy in outputs(stretch):
             copy.wait()
+    for copy in stores:
+        copy.wait()
 
 
 def project(lengths, x, gain, shift, weight, grad, forget_weight, reset_weight, forget_bias, reset_bias):
@@ -251,8 +263,8 @@
             shape((rows_here, width), F32),
             shape((2,) + TILE, F32),
         ),
-        in_specs=[IN_SMEM] + [ANY] * 5 + [IN_VMEM] * 4,
-        out_specs=[ANY] * 8 + [IN_VMEM] * 2,
+        in_specs=[IN_SMEM] + [ANY] * 9,
+        out_specs=[ANY] * 10,
         scratch_shapes=[
             pltpu.VMEM((rows_here, stretches, size, full), BF16),
             pltpu.VMEM((3, full, width), BF16),
@@ -270,8 +282,11 @@
             pltpu.VMEM((2, part, width), BF16),
             pltpu.VMEM((2, part, width), BF16),
             pltpu.VMEM((rows_here,) + TILE, F32),
+            pltpu.VMEM((4,) + TILE, F32),
+            pltpu.VMEM((rows_here, width), F32),
+            pltpu.VMEM((2,) + TILE, F32),
             dma((stretches,)), dma((stretches,)), dma((stretches,)), dma((2,)), dma((2,)), dma((2,)), dma, dma((2,)),
-            dma((8, 2)),
+            dma((8, 2)), dma((6,)),
         ],
         compiler_params=pltpu.CompilerParams(
             collective_id=0, has_side_effects=True, vmem_limit_bytes=VMEM_LIMIT
@@ -300,7 +315,7 @@
 MINE = AT_MIDDLE + 1
 LATE = 3
 PERIOD = 3
-OFFSET = 4
+OFFSET = 3
 MEET = 1
 LEAVE = 2
 KEPT = 3
@@ -308,18 +323,18 @@
 
 
 def finish_kernel(
-    lengths_ref, saved_ref, forget_ref, normed_t_ref, reset_ref, weight_ref, x_ref, mean_ref, scale_ref, pass_ref, gain_ref,
-    forget_weight_ref, reset_weight_ref, sums_ref,
-    total_ref, input_grad_ref, small_ref,
+    lengths_ref, saved_ref, forget_ref, normed_t_ref, reset_ref, weight_ref, x_ref, mean_ref, scale_ref, pass_ref, gain_in,
+    forget_weight_in, reset_weight_in, sums_in,
+    total_ref, input_grad_ref, small_out,
     du, weights, rows_in, mine, core_out, core_in, y_out, y_in, slab_out, slab_in, side_out, side_in, half_out, half_in,
     swap_out, swap_in, cross_out, cross_in,
     ready, dn_own, dn_out, dn_in, moment_own, moment_out, moment_in, x_in, pass_in, mean_in, scale_in, grad_out,
-    norm_sums, keep, saved, forgets, state_s, gate_sums, small_own, small_in, small_z,
+    norm_sums, keep, saved, forgets, state_s, gate_sums, small_own, small_in, small_z, gain_ref, vectors, sums_ref, small_ref,
     load_sem, rows_sem, saved_sem, core_send, core_recv, y_send, y_recv, slab_send, slab_recv, side_send, side_recv,
     half_send, half_recv, swap_send, swap_recv, cross_send, cross_recv, ready_sem,
     gather_send, gather_recv, over_send, over_recv, last_send, last_recv, pair_send, pair_recv, twin_send, twin_recv,
     dn_send, dn_recv, moment_send, moment_recv, norm_sem, grad_sem,
-    small_send, small_recv,
+    small_send, small_recv, vector_sem,
 ):
     device = lax.axis_index("rows")
     devices = lax.axis_size("rows")
@@ -521,7 +536,16 @@
             {"rows": device + (there - z) * z_stride},
         )
 
+    loads = [
+        pltpu.make_async_copy(source, target, vector_sem.at[index])
+        for index, (source, target) in enumerate((
+            (gain_in, gain_ref), (forget_weight_in, vectors.at[0]), (reset_weight_in, vectors.at[1]), (sums_in, sums_ref),
+        ))
+    ]
+    store_small = pltpu.make_async_copy(small_ref, small_out, vector_sem.at[4])
     load_reset.start()
+    for copy in loads:
+        copy.start()
     for copy in load_rows(0):
         copy.start()
     for turn in range(AHEAD - 1):
@@ -567,8 +591,8 @@
     turns = 2 * stretches
     turns_tick = turns // per_gate
     load_reset.wait()
-    for gate in range(3):
-        load_weight(gate).start()
+    for copy in loads:
+        copy.wait()
 
     multiply(0)
     pl.semaphore_wait(barrier, 6)
@@ -725,8 +749,7 @@
 
         @pl.when(t < per_gate)
         def _():
-            forget_weight = forget_weight_ref[...]
-            reset_weight = reset_weight_ref[...]
+            forget_weight, reset_weight = vectors[0], vectors[1]
 
             def back_half(turn, carry):
                 for copy in load_saved(turn):
@@ -787,6 +810,11 @@
             gate_sums[0] = carried[rows_here]
             gate_sums[1] = carried[rows_here + 1]
 
+        for gate in range(3):
+            @pl.when(t == gate)
+            def _():
+                load_weight(gate).start()
+
         @pl.when(t == OFFSET)
         def _():
             for gate in range(3):
@@ -922,6 +950,7 @@
                 small_column(away).wait()
             small_z[z] = small_own[...]
             small_ref[...] = (small_z[0] + small_z[1]) + (small_z[2] + small_z[3])
+            store_small.start()
 
         return carry
 
@@ -930,6 +959,7 @@
         OFFSET + PERIOD * (blocks - 1 + MEET) + 2 * SPLIT + 3 + 2 * HOP,
     )
     lax.fori_loop(0, last, tick, 0)
+    store_small.wait()
 
 
 def finish(
@@ -939,7 +969,6 @@
     full, tokens = normed_t.shape
     rows_here, stretches, size, width = x.shape
     dma = pltpu.SemaphoreType.DMA
-    vmem = IN_VMEM
     norm = NORM_TOKENS
     narrow = width // SPLIT
     pieces = norm // (rows_here * size)
@@ -950,8 +979,8 @@
             jax.ShapeDtypeStruct(x.shape, BF16),
             jax.ShapeDtypeStruct((SUBLANES, width), F32),
         ),
-        in_specs=[IN_SMEM] + [ANY] * 9 + [vmem] * 4,
-        out_specs=(ANY, ANY, vmem),
+        in_specs=[IN_SMEM] + [ANY] * 13,
+        out_specs=(ANY, ANY, ANY),
         scratch_shapes=[
             pltpu.VMEM((3, tokens, width), BF16),
             pltpu.VMEM((3, full, width), BF16),
@@ -992,6 +1021,10 @@
             pltpu.VMEM((SUBLANES, width), F32),
             pltpu.VMEM((2, SUBLANES, width), F32),
             pltpu.VMEM((4, SUBLANES, width), F32),
+            pltpu.VMEM((1, width), F32),
+            pltpu.VMEM((2,) + TILE, F32),
+            pltpu.VMEM((2,) + TILE, F32),
+            pltpu.VMEM((SUBLANES, width), F32),
             dma((4,)), dma((2, 2)), dma((2, AHEAD)),
             dma((2,)), dma((SHORT,)), dma((SHORT,)), dma((RING,)), dma((SHORT,)), dma((LONG,)),
             dma((SHORT,)), dma((LONG,)), dma((SHORT,)), dma((RING,)), dma((SHORT,)), dma((RING,)),
@@ -999,7 +1032,7 @@
             dma((2, LONG)), dma((2, LONG)), dma((LONG,)), dma((LONG,)), dma((LONG,)), dma((LONG,)),
             dma((LONG,)), dma((LONG,)), dma((LONG,)), dma((LONG,)),
             dma((KEPT,)), dma((RING,)), dma((2,)), dma((RING,)), dma((3 + pieces, KEPT)), dma((pieces, 2)),
-            dma((5,)), dma((5,)),
+            dma((5,)), dma((5,)), dma((5,)),
         ],
         compiler_params=pltpu.CompilerParams(
             collective_id=1, has_side_effects=True, vmem_limit_bytes=VMEM_LIMIT
@@ -1010,47 +1043,101 @@
     )
 
 
-COLLECT_STEPS = 8
+COLLECT_PARTS = 4
 
 
 def collect_kernel(
     total_ref, mixed_ref, input_grad_ref, final_ref, small_ref,
-    weight_grad_ref, mixed_out, input_grad_out, final_out, gain_out, shift_out, forget_weight_out, reset_weight_out,
+    weight_grad_ref, mixed_to, input_grad_to, final_out, gain_out, shift_out, forget_weight_out, reset_weight_out,
     forget_bias_out, reset_bias_out,
+    narrow, wide, mixed, input_grad, final, small, vectors, in_sem, out_sem, pass_sem, small_sem, vector_sem,
 ):
-    weight_grad_ref[...] = total_ref[...].astype(F32)
-    mixed_out[...] = mixed_ref[...]
-    input_grad_out[...] = input_grad_ref[...]
-
-    @pl.when(pl.program_id(0) == 0)
-    def _():
-        final_out[...] = final_ref[...]
-        outs = (forget_weight_out, reset_weight_out, forget_bias_out, reset_bias_out, gain_out, shift_out)
-        for index, out in enumerate(outs):
-            out[...] = small_ref[index:index + 1, :].reshape(TILE)
+    gates, full, _ = total_ref.shape
+    rows = full // COLLECT_PARTS
+    parts = [(gate, part) for gate in range(gates) for part in range(COLLECT_PARTS)]
+
+    def take(index):
+        gate, part = parts[index]
+        here = pl.ds(part * rows, rows)
+        return pltpu.make_async_copy(total_ref.at[gate, here], narrow.at[gate, here], in_sem.at[index])
+
+    def give(index):
+        gate, part = parts[index]
+        here = pl.ds(part * rows, rows)
+        return pltpu.make_async_copy(wide.at[gate, here], weight_grad_ref.at[gate, here], out_sem.at[index])
+
+    passed = [
+        (
+            pltpu.make_async_copy(source, held, pass_sem.at[0, index]),
+            pltpu.make_async_copy(held, target, pass_sem.at[1, index]),
+        )
+        for index, (source, held, target) in enumerate(
+            ((mixed_ref, mixed, mixed_to), (input_grad_ref, input_grad, input_grad_to))
+        )
+    ]
+    take_small = pltpu.make_async_copy(small_ref, small, small_sem.at[0])
+    take_final = pltpu.make_async_copy(final_ref, final, small_sem.at[1])
+    give_final = pltpu.make_async_copy(final, final_out, small_sem.at[2])
+    outs = (forget_weight_out, reset_weight_out, forget_bias_out, reset_bias_out, gain_out, shift_out)
+    give_vectors = [
+        pltpu.make_async_copy(vectors.at[index], out, vector_sem.at[index]) for index, out in enumerate(outs)
+    ]
+    take_small.start()
+    take_final.start()
+    for index in range(len(parts)):
+        take(index).start()
+        if index == 1:
+            passed[0][0].start()
+        if index == 3:
+            passed[1][0].start()
+    take_small.wait()
+    for index, copy in enumerate(give_vectors):
+        vectors[index] = small[index:index + 1, :].reshape(TILE)
+        copy.start()
+    take_final.wait()
+    give_final.start()
+    for index, (gate, part) in enumerate(parts):
+        take(index).wait()
+
+        @pl.loop(0, rows // LANES)
+        def _(step):
+            here = pl.ds(aligned(part * rows + step * LANES, LANES), LANES)
+            wide[gate, here, :] = narrow[gate, here, :].astype(F32)
+
+        give(index).start()
+        if index in (2, 4):
+            copies = passed[index // 2 - 1]
+            copies[0].wait()
+            copies[1].start()
+    for index in range(len(parts)):
+        give(index).wait()
+    for copies in passed:
+        copies[1].wait()
+    give_final.wait()
+    for copy in give_vectors:
+        copy.wait()
 
 
 def collect(total, mixed, input_grad, final_state, small):
-    gates, full, width = total.shape
-    total = total.reshape(gates * full, width)
-    mixed, input_grad = (array.reshape(-1, width) for array in (mixed, input_grad))
-    arrays = (total, mixed, input_grad)
-    blocks = [pl.BlockSpec((array.shape[0] // COLLECT_STEPS, width), lambda i: (i, 0)) for array in arrays]
-    whole = lambda *shape: pl.BlockSpec(shape, lambda i: (0,) * len(shape))
     shape = jax.ShapeDtypeStruct
-    weight_grad, *others = pl.pallas_call(
+    dma = pltpu.SemaphoreType.DMA
+    parts = total.shape[0] * COLLECT_PARTS
+    return pl.pallas_call(
         collect_kernel,
-        grid=(COLLECT_STEPS,),
         out_shape=(
             shape(total.shape, F32), shape(mixed.shape, BF16), shape(input_grad.shape, BF16),
             shape(final_state.shape, F32),
         ) + (shape(TILE, F32),) * 6,
-        in_specs=blocks + [whole(*final_state.shape), whole(*small.shape)],
-        out_specs=blocks + [whole(*final_state.shape)] + [whole(*TILE)] * 6,
+        in_specs=[ANY] * 5,
+        out_specs=[ANY] * 10,
+        scratch_shapes=[
+            pltpu.VMEM(total.shape, BF16), pltpu.VMEM(total.shape, F32), pltpu.VMEM(mixed.shape, BF16),
+            pltpu.VMEM(input_grad.shape, BF16), pltpu.VMEM(final_state.shape, F32), pltpu.VMEM(small.shape, F32),
+            pltpu.VMEM((6,) + TILE, F32), dma((parts,)), dma((parts,)), dma((2, 2)), dma((3,)), dma((6,)),
+        ],
         compiler_params=pltpu.CompilerParams(vmem_limit_bytes=VMEM_LIMIT),
         name="collect",
     )(total, mixed, input_grad, final_state, small)
-    return weight_grad.reshape(gates, full, width), *others
 
 
 def on_device(

time: 270 us -> 263 us (0.974)
  Pallas kernels: 269 us -> 262 us
    pallas_call x1, Pallas kernels: 148 us -> 144 us  [finish(): pl.pallas_call(finish_kernel, out_shape=(jax.ShapeDtypeStruct((3, full, w...]
    pallas_call x1, Pallas kernels: 19.6 us -> 16.8 us  [collect(): pl.pallas_call(collect_kernel, out_shape=(shape(total.shape, F32), shape(...]
where the time goes in v5:
time: 263 us; the launch traced here: 262 us
  Pallas kernels  262 us (100%)
    pallas_call x1, Pallas kernels, finish(): pl.pallas_call(finish_kernel, out_shape=(jax.ShapeDtypeStruct((3, full, w...  144 us
    pallas_call x1, Pallas kernels, project(): pl.pallas_call(project_kernel, out_shape=(shape((stretches,) + kept, BF16...  101 us
    pallas_call x1, Pallas kernels, collect(): pl.pallas_call(collect_kernel, out_shape=(shape(total.shape, F32), shape(...  16.8 us

profile of v5, /device:TPU:0, one launch (start us, length us, event | category | flops | bytes accessed | tf_op | source)
XLA Modules:
  0.0 262.5 jit_solution(5913056658973658286)
XLA Ops:
  0.6 100.6 %project.1 = (bf16[16,3,2,32,16,128]{5,4,3,2,1,0:T(8,128)(2,1)}, f32[16,2,64,8,128]{4,3,2,1,0:T(8,128)}, bf16[2048,2048]{1,0:T(8,128)(2,1)}, f32[2048,128]{1,0:T...) custom-call(s32[2,8]{1,0:T(2,128)} %lengths_ref.3, ...), custom_call_target="tpu_custom_call" | custom-call | tf_op jit(solution)/shard_map/project/pallas_call | solution.py:252
  101.2 144.5 %finish.1 = (bf16[3,2048,1024]{2,1,0:T(8,128)(2,1)}, bf16[2,16,64,1024]{3,2,1,0:T(8,128)(2,1)}, f32[8,1024]{1,0:T(8,128)}) custom-call(s32[2,8]{1,0:T(2,128)} %lengths_ref.3, bf16[16,3,2,32,16,128]{5,4,3,2,1,0:T(8,128)(2,1)} %get-tuple-element.33.saved_ref, f32[16,2,64,8,128]{4,3,2,1,0:T(8,128)} %get-tuple-element.34.forget_ref, ...), custom_call_target="tpu_custom_call" | custom-call | tf_op jit(solution)/shard_map/finish/pallas_call | solution.py:975
  245.7 16.8 %collect.1 = (f32[3,2048,1024]{2,1,0:T(8,128)}, bf16[2,16,64,1024]{3,2,1,0:T(8,128)(2,1)}, bf16[2,16,64,1024]{3,2,1,0:T(8,128)(2,1)}, f32[2,1024]{1,0:T(2,128)},...) custom-call(bf16[3,2048,1024]{2,1,0:T(8,128)(2,1)} %get-tuple-elemen, ...), custom_call_target="tpu_custom_call" | custom-call | tf_op jit(solution)/shard_map/collect/pallas_call | solution.py:1125

commit v6 on v5

--- a/solution.py
+++ b/solution.py
@@ -67,10 +67,10 @@
             ),
         )
 
-    def exchange(stretch):
+    def exchange(stretch, row):
         return pltpu.make_async_remote_copy(
-            src_ref=x_ref.at[:, stretch], dst_ref=both.at[:, stretch, :, own_columns],
-            send_sem=send_sem.at[stretch], recv_sem=recv_sem.at[stretch],
+            src_ref=x_ref.at[row, stretch], dst_ref=both.at[row, stretch, :, own_columns],
+            send_sem=send_sem.at[row, stretch], recv_sem=recv_sem.at[row, stretch],
             device_id={"ch": other}, device_id_type=MESH,
         )
 
@@ -81,16 +81,16 @@
         slot = stretch % 2
         return pltpu.make_async_copy(grad_ref.at[:, stretch], grad_in.at[slot], grad_sem.at[slot])
 
-    def outputs(stretch):
+    def outputs(stretch, kinds=slice(None)):
         slot = stretch % 2
         rows = pl.ds(aligned(stretch * tokens, tokens), tokens)
         return tuple(
             pltpu.make_async_copy(source.at[slot], target, out_sem.at[index, slot])
-            for index, (source, target) in enumerate((
-                (saved, saved_ref.at[stretch]), (forget_out, forget_ref.at[stretch]), (normed_t, normed_t_ref.at[:, rows]), (mean_out, mean_ref.at[rows]),
-                (scale_out, scale_ref.at[rows]), (mixed_out, mixed_ref.at[:, stretch]), (pass_out, pass_ref.at[rows]),
-                (reset_out, reset_ref.at[rows]),
-            ))
+            for index, (source, target) in list(enumerate((
+                (normed_t, normed_t_ref.at[:, rows]), (mean_out, mean_ref.at[rows]), (scale_out, scale_ref.at[rows]),
+                (saved, saved_ref.at[stretch]), (forget_out, forget_ref.at[stretch]),
+                (mixed_out, mixed_ref.at[:, stretch]), (pass_out, pass_ref.at[rows]), (reset_out, reset_ref.at[rows]),
+            )))[kinds]
         )
 
     loads = [
@@ -109,7 +109,8 @@
             copy.start()
 
     def begin(stretch, carry):
-        exchange(stretch).start()
+        for row in range(rows_here):
+            exchange(stretch, row).start()
         keep_own(stretch).start()
         return carry
 
@@ -127,7 +128,6 @@
     def work(stretch, carry):
         slot = stretch % 2
         keep_own(stretch).wait()
-        exchange(stretch).wait()
         load_grad(stretch).wait()
 
         @pl.when(stretch + 1 < stretches)
@@ -140,6 +140,8 @@
                 copy.wait()
 
         for row in range(rows_here):
+            exchange(stretch, row).wait()
+
             @pl.loop(0, size // GROUP, unroll=4)
             def _(part):
                 here = pl.ds(aligned(part * GROUP), GROUP)
@@ -161,6 +163,8 @@
         for part in range(full // LANES):
             columns = slice(part * LANES, (part + 1) * LANES)
             normed_t[slot, columns, :] = normed[:, columns].T
+        for copy in outputs(stretch, slice(0, 3)):
+            copy.start()
 
         forget_weight, half_reset_weight, forget_bias, reset_bias = (0.5 * vectors[index] for index in range(4))
 
@@ -220,7 +224,7 @@
             state_s[row] = carried[row]
         sums_ref[0] = carried[rows_here]
         sums_ref[1] = carried[rows_here + 1]
-        for copy in outputs(stretch):
+        for copy in outputs(stretch, slice(3, None)):
             copy.start()
         return carry
 
@@ -285,7 +289,7 @@
             pltpu.VMEM((4,) + TILE, F32),
             pltpu.VMEM((rows_here, width), F32),
             pltpu.VMEM((2,) + TILE, F32),
-            dma((stretches,)), dma((stretches,)), dma((stretches,)), dma((2,)), dma((2,)), dma((2,)), dma, dma((2,)),
+            dma((rows_here, stretches)), dma((rows_here, stretches)), dma((stretches,)), dma((2,)), dma((2,)), dma((2,)), dma, dma((2,)),
             dma((8, 2)), dma((6,)),
         ],
         compiler_params=pltpu.CompilerParams(
@@ -304,7 +308,7 @@
 LONG = 12
 SHORT = 4
 SPLIT = 1
-UNROLL = 4
+UNROLL = 8
 HOP = 2
 CORE = 1
 AT_Y = CORE + HOP
@@ -319,7 +323,7 @@
 MEET = 1
 LEAVE = 2
 KEPT = 3
-AHEAD = 4
+AHEAD = 6
 
 
 def finish_kernel(

time: 263 us -> 262 us (level)
  no operation moved by 1% of the time
where the time goes in v6:
time: 262 us
  Pallas kernels  261 us (100%)
    pallas_call x1, Pallas kernels, finish(): pl.pallas_call(finish_kernel, out_shape=(jax.ShapeDtypeStruct((3, full, w...  144 us
    pallas_call x1, Pallas kernels, project(): pl.pallas_call(project_kernel, out_shape=(shape((stretches,) + kept, BF16...  100 us
    pallas_call x1, Pallas kernels, collect(): pl.pallas_call(collect_kernel, out_shape=(shape(total.shape, F32), shape(...  16.8 us

profile of v6, /device:TPU:0, one launch (start us, length us, event | category | flops | bytes accessed | tf_op | source)
XLA Modules:
  0.0 261.8 jit_solution(5334533263028966340)
XLA Ops:
  0.6 100.4 %project.1 = (bf16[16,3,2,32,16,128]{5,4,3,2,1,0:T(8,128)(2,1)}, f32[16,2,64,8,128]{4,3,2,1,0:T(8,128)}, bf16[2048,2048]{1,0:T(8,128)(2,1)}, f32[2048,128]{1,0:T...) custom-call(s32[2,8]{1,0:T(2,128)} %lengths_ref.3, ...), custom_call_target="tpu_custom_call" | custom-call | tf_op jit(solution)/shard_map/project/pallas_call | solution.py:256
  101.0 143.9 %finish.1 = (bf16[3,2048,1024]{2,1,0:T(8,128)(2,1)}, bf16[2,16,64,1024]{3,2,1,0:T(8,128)(2,1)}, f32[8,1024]{1,0:T(8,128)}) custom-call(s32[2,8]{1,0:T(2,128)} %lengths_ref.3, bf16[16,3,2,32,16,128]{5,4,3,2,1,0:T(8,128)(2,1)} %get-tuple-element.33.saved_ref, f32[16,2,64,8,128]{4,3,2,1,0:T(8,128)} %get-tuple-element.34.forget_ref, ...), custom_call_target="tpu_custom_call" | custom-call | tf_op jit(solution)/shard_map/finish/pallas_call | solution.py:979
  245.0 16.8 %collect.1 = (f32[3,2048,1024]{2,1,0:T(8,128)}, bf16[2,16,64,1024]{3,2,1,0:T(8,128)(2,1)}, bf16[2,16,64,1024]{3,2,1,0:T(8,128)(2,1)}, f32[2,1024]{1,0:T(2,128)},...) custom-call(bf16[3,2048,1024]{2,1,0:T(8,128)(2,1)} %get-tuple-elemen, ...), custom_call_target="tpu_custom_call" | custom-call | tf_op jit(solution)/shard_map/collect/pallas_call | solution.py:1129
